TPU v7x, 256 devices: a whole 4x4x8 slice. The times are simulated.
256 devices in a mesh: blk: 16 (over z, y_hi), img: 16 (over x, y_lo, core).
Axes of the slice: x: 4, y: 4 (y_hi: 2, y_lo: 2; y = y_hi * 2 + y_lo), z: 8, core: 2. Of those that a mesh axis runs over, the one named last changes fastest.
Arguments:
- features: bfloat16 [16384, 768], P(('blk', 'img')), may hold values from -6 to 6
- proj: bfloat16 [768, 768], replicated, may hold values from -0.21875 to 0.21875
- student_text: bfloat16 [16384, 768], P(('blk', 'img')), may hold values from -6 to 6
- teacher_image: bfloat16 [16384, 1024], P(('blk', 'img')), may hold values from -25 to 25
- teacher_text: bfloat16 [16384, 1024], P(('blk', 'img')), may hold values from -5 to 5
Outputs:
- row_loss: float32 [16384], P(('blk', 'img'))
- loss: float32 [], replicated
- grad_proj: float32 [768, 768], P('img')
All inputs are finite; a program needn't handle non-finite values.
Results may differ from a plain program's by a relative error of at most 0.003.
Values may be sent and summed in bfloat16 or wider, within the bound.
No kernel may reach another device: no remote copies, remote signals or barrier semaphores. Data moves between devices by JAX's collectives and lax.ppermute only.
A program may use at most 64 MiB of HBM per device.

v0:
```python
import functools

import jax
import jax.numpy as jnp
import numpy as np
from jax import lax
from jax.experimental import pallas as pl
from jax.experimental.pallas import tpu as pltpu
from jax.sharding import Mesh, PartitionSpec as P

sig_scale = 10.0
sig_bias = -10.0
teacher_gain = 3.0
eps_value = 1e-06

F32 = jnp.float32
BF16 = jnp.bfloat16
LOG2E = float(np.log2(np.e))
LN2 = float(np.log(2.0))
NT = (((1,), (1,)), ((), ()))
ALL = ("z", "yh", "x", "yl", "c")
Y = ("yh", "yl")
VMEM_LIMIT = 8 * 1024 * 1024
FREE = pl.CostEstimate(flops=1, bytes_accessed=1, transcendentals=0)
LANES = 128
STEP = 8
GROUP = 32
PART = 256


def ring(n, k):
    return [(i, (i + k) % n) for i in range(n)]


def flip(n, k):
    return [(i, i ^ k) for i in range(n)]


SMEM = pl.BlockSpec(memory_space=pltpu.SMEM)
VMEM = pl.BlockSpec(memory_space=pltpu.VMEM)


def shape(dims, dtype):
    return jax.ShapeDtypeStruct(dims, dtype)


def params():
    return pltpu.CompilerParams(vmem_limit_bytes=VMEM_LIMIT)


def chip_kernel(place_ref, img_ref, txt_ref, feat2_ref, txt2_ref, timg2_ref, ttxt2_ref, txts_ref, imgs_ref, stxt_ref):
    rows, dt = ttxt2_ref.shape
    half = rows // 2
    mine = pl.ds(pl.multiple_of(place_ref[1] * half, half), half)
    stxt_ref[...] = unit(txt_ref[:, dt:])
    txts_ref[:half, :dt] = txt_ref[mine, :dt]
    txts_ref[half:, :dt] = ttxt2_ref[mine, :]
    txts_ref[:half, dt:] = stxt_ref[mine, :]
    txts_ref[half:, dt:] = unit(txt2_ref[mine, :])
    imgs_ref[:rows, :] = img_ref[...]
    imgs_ref[rows:, :dt] = timg2_ref[...]
    imgs_ref[rows:, dt:] = feat2_ref[...]


def unit(txt):
    txt = txt.astype(F32)
    return (txt / jnp.sqrt(jnp.sum(txt * txt, axis=1, keepdims=True) + eps_value)).astype(BF16)


def column_kernel(a_ref, b_ref, c_ref, d_ref, out_ref):
    rows = a_ref.shape[0]
    for n, ref in enumerate((a_ref, b_ref, c_ref, d_ref)):
        out_ref[n * rows:(n + 1) * rows, :] = ref[...]


def images_kernel(zn, dt, place_ref, own_txt_ref, proj_ref, *refs):
    count = zn // 2 - 1
    img_ref, mine, theirs, last_ref = refs[0], refs[1:1 + count], refs[1 + count:1 + 2 * count], refs[1 + 2 * count]
    timg_ref, feat_ref, simg_ref, simgb_ref, inv_ref, self_ref, diag_ref = refs[2 + 2 * count:]
    rows = img_ref.shape[0] // 2
    z = place_ref[0]
    side = 1 - 2 * place_ref[1]

    def put(ref, shift):
        at = pl.ds(pl.multiple_of(lax.rem(z + shift + zn, zn) * rows, rows), rows)
        timg_ref[at, :] = ref[:rows, :dt]
        feat_ref[at, :] = ref[:rows, dt:]

    put(img_ref, 0)
    for k in range(count):
        put(mine[k], -side * (k + 1))
        put(theirs[k], side * (k + 1))
    put(last_ref, zn // 2)

    def part(p, none):
        some = pl.ds(pl.multiple_of(p * PART, PART), PART)
        pre = jnp.dot(feat_ref[some, :], proj_ref[...], preferred_element_type=F32)
        norm = jnp.sqrt(jnp.sum(pre * pre, axis=1, keepdims=True) + eps_value)
        simg = pre / norm
        simg_ref[some, :] = simg
        simgb_ref[some, :] = simg.astype(BF16)
        inv_ref[some, :] = jnp.broadcast_to(1.0 / norm, (PART, LANES))
        return none

    lax.fori_loop(0, simg_ref.shape[0] // PART, part, 0)
    own = pl.ds(pl.multiple_of(z * rows, rows), rows)
    s = simg_ref[own, :]
    txt = own_txt_ref[...].astype(F32)
    margin = sig_scale * jnp.sum(s.astype(BF16).astype(F32) * txt, axis=1, keepdims=True) + sig_bias
    self_ref[...] = jnp.zeros_like(self_ref)
    lane = lax.broadcasted_iota(jnp.int32, (rows, LANES), 1)
    self_ref[own, :] = jnp.where(lane == 0, -margin, 0.0)
    d = -sig_scale * txt
    diag_ref[...] = (d - s * jnp.sum(s * d, axis=1, keepdims=True)) * inv_ref[own, 0:1]


def make_block(index, last, gain, sizes):
    first = index == 0
    span = sum(sizes)

    def kernel(timg_ref, simgb_ref, old_ref, *refs):
        texts, refs = refs[:len(sizes)], refs[len(sizes):]
        if not first:
            refs = refs[4:]
        te_ref, se_ref, sig_ref, stu_ref, stat_ref, top_ref = refs[:6]
        flat_ref = refs[6] if last else None
        tl, sl = refs[-2:]
        dt = timg_ref.shape[1]
        images = timg_ref.shape[0]
        cols = slice(index * span, (index + 1) * span)
        shrink = float(np.exp(sig_bias))
        fold = lambda v: sum((v[:, k:k + LANES] for k in range(LANES, span, LANES)), v[:, :LANES])
        at = 0
        for ref, n in zip(texts, sizes):
            stu_ref[index * span + at:index * span + at + n, :] = ref[:, dt:]
            at += n
        def part(p, none):
            rows = pl.ds(pl.multiple_of(p * PART, PART), PART)
            at = 0
            for ref, n in zip(texts, sizes):
                tl[rows, at:at + n] = lax.dot_general(timg_ref[rows, :], ref[:, :dt], NT, preferred_element_type=F32)
                sl[rows, at:at + n] = lax.dot_general(simgb_ref[rows, :], ref[:, dt:], NT, preferred_element_type=F32)
                at += n
            return none

        lax.fori_loop(0, images // PART, part, 0)

        def body(k, none):
            for u in range(0, GROUP, 2 * STEP):
                at = pl.multiple_of(k * GROUP + u, 2 * STEP)
                outs = []
                for half in range(2):
                    rows = pl.ds(pl.multiple_of(at + half * STEP, STEP), STEP)
                    t = (gain * LOG2E) * tl[rows, :]
                    s = (sig_scale * LOG2E) * sl[rows, :]
                    top = jnp.max(t, axis=1, keepdims=True)
                    if not first:
                        top = jnp.maximum(top, old_ref[rows, :LANES])
                    top = jnp.broadcast_to(top, (STEP, LANES))
                    te = jnp.exp2(t - jnp.concatenate([top] * (span // LANES), axis=1))
                    se = jnp.exp2(s)
                    em = se * shrink
                    up = 1.0 + em
                    sig = em * pl.reciprocal(up, approx=True)
                    soft = jnp.log(up) + (em - (up - 1.0))
                    outs.append((te, se, sig))
                    sums = [fold(te), fold(se), fold(te * (t - s)), fold(soft)]
                    if first:
                        sums[3] = sums[3] + old_ref[rows, :]
                    else:
                        w = jnp.exp2(old_ref[rows, :LANES] - top)
                        was = [old_ref[rows, j * LANES:(j + 1) * LANES] for j in range(1, 5)]
                        sums = [sums[0] + w * was[0], sums[1] + was[1], sums[2] + w * was[2], sums[3] + was[3]]
                    top_ref[rows, :] = top
                    for j, v in enumerate([top] + sums):
                        stat_ref[rows, j * LANES:(j + 1) * LANES] = v
                for ref, low, high in zip((te_ref, se_ref, sig_ref), *outs):
                    ref[pl.ds(at, 2 * STEP), cols] = jnp.concatenate([low, high], axis=0).astype(BF16)
            return none

        lax.fori_loop(0, images // GROUP, body, 0)
        if last:
            ones = jnp.ones((8, LANES), F32)
            out = [stat_ref[:, :LANES].T[:1, :]]
            for k in range(1, 5):
                v = lax.dot_general(ones, stat_ref[:, k * LANES:(k + 1) * LANES], NT, precision=lax.Precision.HIGHEST, preferred_element_type=F32)
                out.append(v[:1, :])
            flat_ref[...] = jnp.concatenate(out + [jnp.zeros((3, images), F32)], axis=0)

    return kernel


def carry(weights, txt, simg, inv):
    d = jnp.dot(weights, txt, preferred_element_type=F32)
    along = jnp.sum(simg * d, axis=1, keepdims=True)
    return ((d - simg * along) * inv).astype(BF16)


def student_kernel(se_ref, sig_ref, stu_ref, simg_ref, inv_ref, feat_ref, a_ref, c_ref, ft_ref, done_ref):
    def part(p, none):
        rows = pl.ds(pl.multiple_of(p * PART, PART), PART)
        for src, dst in ((se_ref, a_ref), (sig_ref, c_ref)):
            dst[rows, :] = carry(src[rows, :], stu_ref[...], simg_ref[rows, :], inv_ref[rows, 0:1])
        return none

    lax.fori_loop(0, se_ref.shape[0] // PART, part, 0)
    ft_ref[...] = feat_ref[...].T
    done_ref[...] = jnp.zeros_like(done_ref)


def teacher_kernel(te_ref, stu_ref, simg_ref, inv_ref, *refs):
    stats, (b_ref, scaled) = refs[:-2], refs[-2:]
    span = te_ref.shape[1] // len(stats)

    def part(p, none):
        rows = pl.ds(pl.multiple_of(p * PART, PART), PART)
        top = stats[-1][rows, 0:1]
        for n, stat in enumerate(stats):
            cols = slice(n * span, (n + 1) * span)
            w = jnp.exp2(stat[rows, 0:1] - top)
            scaled[rows, cols] = (te_ref[rows, cols].astype(F32) * w).astype(BF16)
        b_ref[rows, :] = carry(scaled[rows, :], stu_ref[...], simg_ref[rows, :], inv_ref[rows, 0:1])
        return none

    lax.fori_loop(0, te_ref.shape[0] // PART, part, 0)


def away_kernel(place_ref, window_ref, ahead_ref, behind_ref, flat_ref, a_ref, b_ref, c_ref, diag_ref, ft_ref,
                out_ref, hi_ref, lo_ref, val_ref, turned, cut_ft):
    rows = diag_ref.shape[0]
    half, ds = cut_ft.shape[0], a_ref.shape[1]
    sums = merge(window_ref[...], ahead_ref[...], behind_ref[...])
    top, tsum, ssum, tval, soft = (sums[k:k + 1, :] for k in range(5))
    value = tval / tsum * LN2 + soft - (top * LN2 + jnp.log(tsum)) + jnp.log(ssum)
    val_ref[...] = jnp.broadcast_to(value, val_ref.shape)
    ca = sig_scale / ssum
    cb = -sig_scale * jnp.exp2(flat_ref[0:1, :] - top) / tsum
    row = lax.broadcasted_iota(jnp.int32, (LANES, ca.shape[1]), 0)
    turned[...] = jnp.where(row == 0, ca, cb).T

    def part(p, none):
        some = pl.ds(pl.multiple_of(p * LANES, LANES), LANES)
        d = turned[some, 0:1] * a_ref[some, :].astype(F32) + turned[some, 1:2] * b_ref[some, :].astype(F32)
        d = d + sig_scale * c_ref[some, :].astype(F32)
        hi = d.astype(BF16)
        hi_ref[some, :] = hi
        lo_ref[some, :] = (d - hi.astype(F32)).astype(BF16)
        return none

    lax.fori_loop(0, hi_ref.shape[0] // LANES, part, 0)
    own = pl.ds(pl.multiple_of(place_ref[0] * rows, rows), rows)
    mine = hi_ref[own, :].astype(F32) + lo_ref[own, :].astype(F32) + diag_ref[...]
    mine_hi = mine.astype(BF16)
    hi_ref[own, :] = mine_hi
    lo_ref[own, :] = (mine - mine_hi.astype(F32)).astype(BF16)
    pick(cut_ft, ft_ref, 1 - place_ref[1])
    g = jnp.dot(cut_ft[...], hi_ref[...], preferred_element_type=F32)
    out_ref[:half, :] = g + jnp.dot(cut_ft[...], lo_ref[...], preferred_element_type=F32)
    out_ref[half:, :] = jnp.broadcast_to(jnp.sum(value, axis=1, keepdims=True), (8, ds))


def pick(dst, src, core):
    groups = 8
    cut = dst.shape[0] // groups
    for g in range(groups):
        dst[g * cut:(g + 1) * cut, :] = src[pl.ds(pl.multiple_of((2 * g + core) * cut, cut), cut), :]


def home_kernel(place_ref, ft_ref, hi_ref, lo_ref, out_ref, cut_ft):
    pick(cut_ft, ft_ref, place_ref[1])
    out_ref[...] = jnp.dot(cut_ft[...], hi_ref[...], preferred_element_type=F32) + jnp.dot(
        cut_ft[...], lo_ref[...], preferred_element_type=F32)


def packed(loss):
    hi = loss.astype(BF16).astype(F32)
    mid = (loss - hi).astype(BF16).astype(F32)
    low = loss - hi - mid
    row = lax.broadcasted_iota(jnp.int32, loss.shape, 0)
    out = jnp.where(row == 0, hi, jnp.where(row == 1, mid, jnp.where(row == 2, low, 0.0)))
    return jnp.concatenate([out, jnp.zeros_like(out)], axis=0).astype(BF16)


def unpacked(rows):
    rows = rows.astype(F32)
    return rows[0:1, :] + rows[1:2, :] + rows[2:3, :]


def cores_kernel(xn, place_ref, home_ref, got_ref, away_ref, keep_ref, *sends):
    half = home_ref.shape[0]
    cut = half // xn
    loss = got_ref[half:, :] + away_ref[half:, :]
    x = place_ref[2]
    at = pl.ds(pl.multiple_of(x * cut, cut), cut)
    keep_ref[:cut, :] = home_ref[at, :] + got_ref[at, :]
    keep_ref[cut:, :] = loss
    rows = packed(loss)
    for k, ref in zip((1, 3, 2), sends):
        at = pl.ds(pl.multiple_of(lax.rem(x + k, xn) * cut, cut), cut)
        ref[:cut, :] = (home_ref[at, :] + got_ref[at, :]).astype(BF16)
        ref[cut:, :] = rows


def rows_kernel(place_ref, keep_ref, p_ref, q_ref, r_ref, mine_ref, across_ref, other_ref, total):
    cut = keep_ref.shape[0] - 8
    half = cut // 2
    total[...] = keep_ref[:cut, :]
    loss = keep_ref[cut:, :]
    for ref in (p_ref, q_ref, r_ref):
        total[...] += ref[:cut, :].astype(F32)
        loss = loss + unpacked(ref[cut:, :])
    y = place_ref[3]
    mine_ref[:half, :] = total[pl.ds(pl.multiple_of(y * half, half), half), :]
    mine_ref[half:, :] = loss
    across_ref[:half, :] = mine_ref[:half, :].astype(BF16)
    across_ref[half:, :] = packed(loss)
    other_ref[:half, :] = total[pl.ds(pl.multiple_of((1 - y) * half, half), half), :]
    other_ref[half:, :] = loss


def plane_kernel(mine_ref, p_ref, q_ref, r_ref, out_ref, loss_ref):
    half = out_ref.shape[0]
    out_ref[...] = mine_ref[:half, :] + p_ref[:half, :] + q_ref[:half, :] + r_ref[:half, :].astype(F32)
    loss = mine_ref[half:, :] + p_ref[half:, :] + q_ref[half:, :] + unpacked(r_ref[half:, :])
    loss_ref[...] = loss[:, :LANES]


def merge(*parts):
    top = functools.reduce(jnp.maximum, [p[0:1, :] for p in parts])
    out = [0.0] * 4
    for p in parts:
        w = jnp.exp2(p[0:1, :] - top)
        out = [out[0] + w * p[1:2, :], out[1] + p[2:3, :], out[2] + w * p[3:4, :], out[3] + p[4:5, :]]
    return jnp.concatenate([top] + out + [jnp.zeros((3, top.shape[1]), F32)], axis=0)


def near_kernel(own_ref, above_ref, below_ref, after_ref, pair_ref, window_ref):
    pair = merge(own_ref[...], above_ref[...])
    pair_ref[...] = pair
    window_ref[...] = merge(pair, below_ref[...])


def per_device(features, proj, student_text, teacher_image, teacher_text):
    rows, feat = features.shape
    dt = teacher_text.shape[1]
    ds = student_text.shape[1]
    zn, yn, xn, cn = (lax.axis_size(a) for a in ("z", Y, "x", "c"))
    images = rows * zn
    batch = images * yn * xn * cn
    texts = rows * yn * xn * cn
    column = rows * yn
    gain = float(teacher_gain / np.sqrt(np.float32(dt)))
    half = feat // cn
    place = jnp.stack([lax.axis_index(a) for a in ("z", "c", "x", "yl")]).astype(jnp.int32)

    swap = lambda v: lax.ppermute(v, "c", flip(cn, 1))
    raw = (features, student_text, teacher_image, teacher_text)
    img = jnp.concatenate([teacher_image, features], axis=1)
    txt = jnp.concatenate([teacher_text, student_text], axis=1)
    txts, imgs, st_own = pl.pallas_call(
        chip_kernel,
        in_specs=[SMEM] + [VMEM] * 6,
        out_specs=[VMEM] * 3,
        out_shape=[shape((rows, dt + ds), BF16), shape((2 * rows, dt + feat), BF16), shape((rows, ds), BF16)],
        compiler_params=params(),
        cost_estimate=FREE,
        name="chip",
    )(place, img, txt, *(swap(v) for v in raw))

    def plane(v, step, stage):
        pairs = []
        dims = (yn // 2, xn, 2, cn)
        for src in np.ndindex(*dims):
            yh, x, yl, c = src
            y = 2 * yh + yl
            if c == stage:
                y = (y + step) % yn
            else:
                x = (x + step) % xn
            dst = (y // 2, x, y % 2, c)
            pairs.append((int(np.ravel_multi_index(src, dims)), int(np.ravel_multi_index(dst, dims))))
        return lax.ppermute(v, ("yh", "x", "yl", "c"), pairs)

    def climb(v, step):
        pairs = [(z * cn + c, (z + (step if c == 0 else -step)) % zn * cn + c) for z in range(zn) for c in range(cn)]
        return lax.ppermute(v, ("z", "c"), pairs)

    together = lax.optimization_barrier
    left, right, far, one, two = together((plane(txts, 1, 0), plane(txts, -1, 0), plane(txts, 2, 0), climb(imgs, 1), climb(imgs, 2)))
    own_col = pl.pallas_call(
        column_kernel,
        in_specs=[VMEM] * 4,
        out_specs=VMEM,
        out_shape=shape((column, dt + ds), BF16),
        compiler_params=params(),
        name="column",
    )(txts, left, right, far)
    left_col, right_col = plane(own_col, 1, 1), plane(own_col, -1, 1)
    far_col = plane(left_col, 1, 1)
    three = climb(one, 2)
    four = climb(two[:rows], 2)
    mine = [one, two, three]
    theirs = [swap(v[rows:]) for v in mine]

    timg, feats, simg, simgb, inv, self_col, diag = pl.pallas_call(
        functools.partial(images_kernel, zn, dt),
        in_specs=[SMEM] + [VMEM] * (4 + 2 * len(mine)),
        out_specs=[VMEM] * 7,
        out_shape=[shape((images, dt), BF16), shape((images, feat), BF16), shape((images, ds), F32), shape((images, ds), BF16),
                   shape((images, LANES), F32), shape((images, LANES), F32), shape((rows, ds), F32)],
        compiler_params=params(),
        cost_estimate=FREE,
        name="images",
    )(place, st_own, proj, imgs, *mine, *theirs, four)

    blocks = [(own_col, swap(own_col)), (left_col, swap(left_col)), (right_col, swap(right_col)), None]
    span = column * cn
    stat = self_col
    chain = []
    stats = []
    for n, block in enumerate(blocks):
        final = n == len(blocks) - 1
        if final:
            block = (far_col, swap(far_col))
        big = [shape((images, texts), BF16)] * 3 + [shape((texts, ds), BF16), shape((images, 5 * LANES), F32), shape((images, LANES), F32)]
        out = pl.pallas_call(
            make_block(n, final, gain, [v.shape[0] for v in block]),
            in_specs=[VMEM] * (3 + len(block) + len(chain)),
            out_specs=[VMEM] * (7 if final else 6),
            out_shape=big + ([shape((8, images), F32)] if final else []),
            scratch_shapes=[pltpu.VMEM((images, span), F32)] * 2,
            input_output_aliases={3 + len(block) + k: k for k in range(len(chain))} | ({2: 4} if n else {}),
            compiler_params=params(),
            cost_estimate=FREE,
            name="block" + str(n),
        )(timg, simgb, stat, *block, *chain)
        chain, stat = list(out[:4]), out[4]
        stats.append(out[5])
        if n == 1:
            far_col, stat = together((far_col, stat))
    flat = out[6]
    te, se, sig, stu = chain

    a, c, ft, done_student = pl.pallas_call(
        student_kernel,
        in_specs=[VMEM] * 6,
        out_specs=[VMEM] * 4,
        out_shape=[shape((images, ds), BF16)] * 2 + [shape((feat, images), BF16), shape((8, LANES), F32)],
        compiler_params=params(),
        cost_estimate=FREE,
        name="student",
    )(se, sig, stu, simg, inv, feats)
    b = pl.pallas_call(
        teacher_kernel,
        in_specs=[VMEM] * (4 + len(stats)),
        out_specs=VMEM,
        out_shape=shape((images, ds), BF16),
        scratch_shapes=[pltpu.VMEM((images, texts), BF16)],
        compiler_params=params(),
        cost_estimate=FREE,
        name="teacher",
    )(te, stu, simg, inv, *stats)

    below = lax.ppermute(flat, "z", ring(zn, 1))
    above = lax.ppermute(flat, "z", ring(zn, zn - 1))
    pair, window = pl.pallas_call(
        near_kernel,
        in_specs=[VMEM] * 4,
        out_specs=[VMEM] * 2,
        out_shape=[shape((8, images), F32)] * 2,
        compiler_params=params(),
        name="near",
    )(flat, above, below, done_student)
    ahead = lax.ppermute(window, "z", ring(zn, zn - 3))
    behind = lax.ppermute(pair, "z", ring(zn, 3))

    away, hi, lo, val = pl.pallas_call(
        away_kernel,
        in_specs=[SMEM] + [VMEM] * 9,
        out_specs=[VMEM] * 4,
        out_shape=[shape((half + 8, ds), F32), shape((images, ds), BF16), shape((images, ds), BF16), shape((8, images), F32)],
        scratch_shapes=[pltpu.VMEM((images, LANES), F32), pltpu.VMEM((half, images), BF16)],
        compiler_params=params(),
        cost_estimate=FREE,
        name="away",
    )(place, window, ahead, behind, flat, a, b, c, diag, ft)
    arrived = swap(away)
    home = pl.pallas_call(
        home_kernel,
        in_specs=[SMEM] + [VMEM] * 3,
        out_specs=VMEM,
        out_shape=shape((half, ds), F32),
        scratch_shapes=[pltpu.VMEM((half, images), BF16)],
        compiler_params=params(),
        cost_estimate=FREE,
        name="home",
    )(place, ft, hi, lo)

    cut = half // xn
    keep, *sends = pl.pallas_call(
        functools.partial(cores_kernel, xn),
        in_specs=[SMEM] + [VMEM] * 3,
        out_specs=[VMEM] * 4,
        out_shape=[shape((cut + 8, ds), F32)] + [shape((cut + 16, ds), BF16)] * 3,
        compiler_params=params(),
        name="cores",
    )(place, home, arrived, away)
    got = [lax.ppermute(v, "x", ring(xn, k)) for k, v in zip((1, 3, 2), sends)]
    cut = cut // 2
    mine, across, other = pl.pallas_call(
        rows_kernel,
        in_specs=[SMEM] + [VMEM] * 4,
        out_specs=[VMEM] * 3,
        out_shape=[shape((cut + 8, ds), F32), shape((cut + 16, ds), BF16), shape((cut + 8, ds), F32)],
        scratch_shapes=[pltpu.VMEM((2 * cut, ds), F32)],
        compiler_params=params(),
        name="rows",
    )(place, keep, *got)
    own, loss = pl.pallas_call(
        plane_kernel,
        in_specs=[VMEM] * 4,
        out_specs=[VMEM] * 2,
        out_shape=[shape((cut, ds), F32), shape((8, LANES), F32)],
        compiler_params=params(),
        name="plane",
    )(mine, lax.ppermute(other, Y, ring(yn, 1)), lax.ppermute(other, Y, ring(yn, 3)), lax.ppermute(across, Y, ring(yn, 2)))

    below = lax.ppermute(own, "z", ring(zn, 1))
    above = lax.ppermute(own, "z", ring(zn, zn - 1))
    pair = own + above
    window = pair + below
    ahead = lax.ppermute(window.astype(BF16), "z", ring(zn, zn - 3))
    behind = lax.ppermute(pair.astype(BF16), "z", ring(zn, 3))
    grad = window + ahead.astype(F32) + behind.astype(F32)

    row_loss = lax.dynamic_slice_in_dim(val[0], lax.axis_index("z") * rows, rows, 0)
    return (row_loss, loss[0, 0] / batch, grad)


def solution(mesh):
    sizes = dict(mesh.shape)
    fine = Mesh(np.asarray(mesh.devices).reshape(sizes["blk"] // 2, 2, sizes["img"] // 4, 2, 2), ALL)
    return jax.shard_map(
        per_device,
        mesh=fine,
        in_specs=(P(ALL, None), P(), P(ALL, None), P(ALL, None), P(ALL, None)),
        out_specs=(P(ALL), P(), P(("x", "yl", "c"), None)),
        check_vma=False,
    )
```

profile of v0, /device:TPU:2, one launch (start us, length us, event | category | flops | bytes accessed | tf_op | source)
XLA Modules:
  0.0 130.9 jit_solution(2525851634303509630)
XLA Ops:
  5.6 3.3 %collective-permute-start.8 = (bf16[128,1792]{1,0:T(8,128)(2,1)S(1)}, bf16[128,1792]{1,0:T(8,128)(2,1)S(1)}, u32[]{:S(2)}, u32[]{:S(2)}) collective-permute-start(bf16[128,1792]{1,0:T(8,128)(2,1)S(1)} %get-tuple-element.64.refs_0_), channel_id=1, source_target_pairs={{0,64},{1,193},{32,96},{33,225},{64,128},{65,1},{96,160},{97,33},{... | collective-permute-start | bytes 1376264 | tf_op jit(solution)/shard_map/ppermute | solution.py:386
  16.5 3.3 %collective-permute-done.6.d_ref = bf16[64,1792]{1,0:T(8,128)(2,1)S(1)} collective-permute-done((bf16[64,1792]{1,0:T(8,128)(2,1)S(1)}, bf16[64,1792]{1,0:T(8,128)(2,1)S(1)}, u32[]{:S(2)}, u32[]{:S(2)}) %collective-permute-start.6) | collective-permute-done | bytes 229408 | tf_op jit(solution)/shard_map/ppermute | solution.py:382
  19.8 3.1 %collective-permute-done.8.refs_2_ = bf16[128,1792]{1,0:T(8,128)(2,1)S(1)} collective-permute-done((bf16[128,1792]{1,0:T(8,128)(2,1)S(1)}, bf16[128,1792]{1,0:T(8,128)(2,1)S(1)}, u32[]{:S(2)}, u32[]{:S(2)}) %collective-permute-start.8) | collective-permute-done | bytes 458784 | tf_op jit(solution)/shard_map/ppermute | solution.py:386
  26.4 2.3 %collective-permute-start.13 = (bf16[64,1792]{1,0:T(8,128)(2,1)S(1)}, bf16[64,1792]{1,0:T(8,128)(2,1)S(1)}, u32[]{:S(2)}, u32[]{:S(2)}) collective-permute-start(bf16[64,1792]{1,0:T(8,128)(2,1)S(1)} %get-tuple-element.123), channel_id=1, source_target_pairs={{0,64},{1,193},{32,96},{33,225},{64,128},{65,1},{96,160},{97,33},{... | collective-permute-start | bytes 688136 | tf_op jit(solution)/shard_map/ppermute | solution.py:386
  28.8 2.6 %collective-permute-start.9 = (bf16[128,1792]{1,0:T(8,128)(2,1)S(1)}, bf16[128,1792]{1,0:T(8,128)(2,1)S(1)}, u32[]{:S(2)}, u32[]{:S(2)}) collective-permute-start(bf16[128,1792]{1,0:T(8,128)(2,1)S(1)} %collective-permute-done.7.refs_1_), channel_id=1, source_target_pairs={{0,64},{1,193},{32,96},{33,225},{64,128},{65,1},{96,160},{97,33},{... | collective-permute-start | bytes 1376264 | tf_op jit(solution)/shard_map/ppermute | solution.py:386
  33.9 2.6 %collective-permute-done.14.refs_0_ = bf16[256,1792]{1,0:T(8,128)(2,1)S(1)} collective-permute-done((bf16[256,1792]{1,0:T(8,128)(2,1)S(1)}, bf16[256,1792]{1,0:T(8,128)(2,1)S(1)}, u32[]{:S(2)}, u32[]{:S(2)}) %collective-permute-start.14) | collective-permute-done | bytes 917536 | tf_op jit(solution)/shard_map/ppermute | solution.py:382
  36.5 2.3 %collective-permute-start.17 = (bf16[256,1792]{1,0:T(8,128)(2,1)S(1)}, bf16[256,1792]{1,0:T(8,128)(2,1)S(1)}, u32[]{:S(2)}, u32[]{:S(2)}) collective-permute-start(bf16[256,1792]{1,0:T(8,128)(2,1)S(1)} %collective-permute-done.14.refs_0_), channel_id=1, source_target_pairs={{0,1},{1,0},{2,3},{3,2},{4,5},{5,4},{6,7},{7,6},{8,9},{9,8},{10,11... | collective-permute-start | bytes 2752520 | tf_op jit(solution)/shard_map/ppermute | solution.py:356
  41.0 4.8 %collective-permute-start.10 = (bf16[64,1792]{1,0:T(8,128)(2,1)S(1)}, bf16[64,1792]{1,0:T(8,128)(2,1)S(1)}, u32[]{:S(2)}, u32[]{:S(2)}) collective-permute-start(bf16[64,1792]{1,0:T(8,128)(2,1)S(1)} %slice.18), channel_id=1, source_target_pairs={{0,1},{1,0},{2,3},{3,2},{4,5},{5,4},{6,7},{7,6},{8,9},{9,8},{10,11... | collective-permute-start | bytes 688136 | tf_op jit(solution)/shard_map/ppermute | solution.py:356
  50.9 3.2 %block0.1 = (bf16[512,2048]{1,0:T(8,128)(2,1)S(1)}, bf16[512,2048]{1,0:T(8,128)(2,1)S(1)}, bf16[512,2048]{1,0:T(8,128)(2,1)S(1)}, bf16[2048,768]{1,0:T(8,128)(2,...) custom-call(bf16[512,1024]{1,0:T(8,128)(2,1)S(1)} %get-tuple-element.68.timg_ref, ...), custom_call_target="tpu_custom_call" | custom-call | flops 1 | bytes 1 | tf_op jit(solution)/shard_map/block0/pallas_call | solution.py:426
  54.1 3.6 %block1.1 = (bf16[512,2048]{1,0:T(8,128)(2,1)S(1)}, bf16[512,2048]{1,0:T(8,128)(2,1)S(1)}, bf16[512,2048]{1,0:T(8,128)(2,1)S(1)}, bf16[2048,768]{1,0:T(8,128)(2,...) custom-call(bf16[512,1024]{1,0:T(8,128)(2,1)S(1)} %get-tuple-element, ...), custom_call_target="tpu_custom_call", output_to_operand_aliasing={{0}: (5, {}), {1}: (6, {}), {2}: (7, {}), {3}: (8, {}), {4}... | custom-call | flops 1 | bytes 1 | tf_op jit(solution)/shard_map/block1/pallas_call | solution.py:426
  57.9 3.6 %block2.1 = (bf16[512,2048]{1,0:T(8,128)(2,1)S(1)}, bf16[512,2048]{1,0:T(8,128)(2,1)S(1)}, bf16[512,2048]{1,0:T(8,128)(2,1)S(1)}, bf16[2048,768]{1,0:T(8,128)(2,...) custom-call(bf16[512,1024]{1,0:T(8,128)(2,1)S(1)} %get-tuple-element, ...), custom_call_target="tpu_custom_call", output_to_operand_aliasing={{0}: (5, {}), {1}: (6, {}), {2}: (7, {}), {3}: (8, {}), {4}... | custom-call | flops 1 | bytes 1 | tf_op jit(solution)/shard_map/block2/pallas_call | solution.py:426
  61.6 4.6 %block3.1 = (bf16[512,2048]{1,0:T(8,128)(2,1)S(1)}, bf16[512,2048]{1,0:T(8,128)(2,1)S(1)}, bf16[512,2048]{1,0:T(8,128)(2,1)S(1)}, bf16[2048,768]{1,0:T(8,128)(2,...) custom-call(bf16[512,1024]{1,0:T(8,128)(2,1)S(1)} %get-tuple-element, ...), custom_call_target="tpu_custom_call", output_to_operand_aliasing={{0}: (5, {}), {1}: (6, {}), {2}: (7, {}), {3}: (8, {}), {4}... | custom-call | flops 1 | bytes 1 | tf_op jit(solution)/shard_map/block3/pallas_call | solution.py:426
  66.2 3.9 %collective-permute-start.21 = (f32[8,512]{1,0:T(8,128)S(1)}, f32[8,512]{1,0:T(8,128)S(1)}, u32[]{:S(2)}, u32[]{:S(2)}) collective-permute-start(f32[8,512]{1,0:T(8,128)S(1)} %get-tuple-element.91.own_ref.flat_ref), channel_id=1, source_target_pairs={{0,224},{32,0},{64,32},{96,64},{128,96},{160,128},{192,160},{224,1... | collective-permute-start | bytes 49160 | tf_op jit(solution)/shard_map/ppermute | solution.py:465
  70.1 4.1 %student.1 = (bf16[512,768]{1,0:T(8,128)(2,1)S(1)}, bf16[512,768]{1,0:T(8,128)(2,1)S(1)}, bf16[768,512]{1,0:T(8,128)(2,1)S(1)}, f32[8,128]{1,0:T(8,128)S(1)}) custom-call(bf16[512,2048]{1,0:T(8,128)(2,1)S(1)} %get-tuple-element.92.se_ref, bf16[512,2048]{1,0:T(8,128)(2,1)S(1)} %get-tuple-element.93.sig_ref, bf16[2048,768]{1,0:T(8,128)(2,1)S(1)} %get-tuple-element.94.stu_ref, ...), custom_call_target="tpu_custom_call" | custom-call | flops 1 | bytes 1 | tf_op jit(solution)/shard_map/student/pallas_call | solution.py:444
  75.1 3.0 %collective-permute-start.23 = (f32[8,512]{1,0:T(8,128)S(1)}, f32[8,512]{1,0:T(8,128)S(1)}, u32[]{:S(2)}, u32[]{:S(2)}) collective-permute-start(f32[8,512]{1,0:T(8,128)S(1)} %get-tuple-element.99.window_ref), channel_id=1, source_target_pairs={{0,160},{32,192},{64,224},{96,0},{128,32},{160,64},{192,96},{224,1... | collective-permute-start | bytes 49160 | tf_op jit(solution)/shard_map/ppermute | solution.py:474
  79.0 2.4 %teacher.1.b_ref = bf16[512,768]{1,0:T(8,128)(2,1)S(1)} custom-call(bf16[512,2048]{1,0:T(8,128)(2,1)S(1)} %get-tuple-element.102.te_ref, bf16[2048,768]{1,0:T(8,128)(2,1)S(1)} %get-tuple-element.94.stu_ref, f32[512,768]{1,0:T(8,128)S(1)} %get-tuple-element.95.simg_ref, f32[512,128]{1,0:T(8,128)S(1)} %get-tuple-element.96.inv_ref, ...), custom_call_target="tpu_custom_call" | custom-call | flops 1 | bytes 1 | tf_op jit(solution)/shard_map/teacher/pallas_call | solution.py:453
  81.4 3.5 %collective-permute-done.24.behind_ref = f32[8,512]{1,0:T(8,128)S(1)} collective-permute-done((f32[8,512]{1,0:T(8,128)S(1)}, f32[8,512]{1,0:T(8,128)S(1)}, u32[]{:S(2)}, u32[]{:S(2)}) %collective-permute-start.24) | collective-permute-done | bytes 16416 | tf_op jit(solution)/shard_map/ppermute | solution.py:475
  84.9 2.3 %away.1 = (f32[392,768]{1,0:T(8,128)S(1)}, bf16[512,768]{1,0:T(8,128)(2,1)S(1)}, bf16[512,768]{1,0:T(8,128)(2,1)S(1)}, f32[8,512]{1,0:T(8,128)S(1)}) custom-call(s32[4]{0:T(128)S(1)} %pad_add_fusion.place_ref, f32[8,512]{1,0:T(8,128)S(1)} %get-tuple-element.99.window_ref, f32[8,512]{1,0:T(8,128)S(1)} %collective-permute-done.23.ahead_ref, ...), custom_call_target="tpu_custom_call" | custom-call | flops 1 | bytes 1 | tf_op jit(solution)/shard_map/away/pallas_call | solution.py:477
  95.2 3.2 %collective-permute-done.26.p_ref = bf16[112,768]{1,0:T(8,128)(2,1)S(1)} collective-permute-done((bf16[112,768]{1,0:T(8,128)(2,1)S(1)}, bf16[112,768]{1,0:T(8,128)(2,1)S(1)}, u32[]{:S(2)}, u32[]{:S(2)}) %collective-permute-start.26) | collective-permute-done | bytes 172064 | tf_op jit(solution)/shard_map/ppermute | solution.py:508
  99.2 3.8 %collective-permute-done.28.r_ref = bf16[112,768]{1,0:T(8,128)(2,1)S(1)} collective-permute-done((bf16[112,768]{1,0:T(8,128)(2,1)S(1)}, bf16[112,768]{1,0:T(8,128)(2,1)S(1)}, u32[]{:S(2)}, u32[]{:S(2)}) %collective-permute-start.28) | collective-permute-done | bytes 172064 | tf_op jit(solution)/shard_map/ppermute | solution.py:508
  108.7 4.4 %collective-permute-done.31.r_ref = bf16[64,768]{1,0:T(8,128)(2,1)S(1)} collective-permute-done((bf16[64,768]{1,0:T(8,128)(2,1)S(1)}, bf16[64,768]{1,0:T(8,128)(2,1)S(1)}, u32[]{:S(2)}, u32[]{:S(2)}) %collective-permute-start.31) | collective-permute-done | bytes 98336 | tf_op jit(solution)/shard_map/ppermute | solution.py:526
  115.3 3.1 %collective-permute-done.32 = f32[48,768]{1,0:T(8,128)S(1)} collective-permute-done((f32[48,768]{1,0:T(8,128)S(1)}, f32[48,768]{1,0:T(8,128)S(1)}, u32[]{:S(2)}, u32[]{:S(2)}) %collective-permute-start.32) | collective-permute-done | bytes 147488 | tf_op jit(solution)/shard_map/ppermute | solution.py:529
  120.9 2.7 %collective-permute-start.35 = (bf16[48,768]{1,0:T(8,128)(2,1)S(1)}, bf16[48,768]{1,0:T(8,128)(2,1)S(1)}, u32[]{:S(2)}, u32[]{:S(2)}) collective-permute-start(bf16[48,768]{1,0:T(8,128)(2,1)S(1)} %get-tuple-element.126), channel_id=1, source_target_pairs={{0,96},{32,128},{64,160},{96,192},{128,224},{160,0},{192,32},{224,... | collective-permute-start | bytes 221192 | tf_op jit(solution)/shard_map/ppermute | solution.py:533
  126.0 3.1 %collective-permute-done.35 = bf16[48,768]{1,0:T(8,128)(2,1)S(1)} collective-permute-done((bf16[48,768]{1,0:T(8,128)(2,1)S(1)}, bf16[48,768]{1,0:T(8,128)(2,1)S(1)}, u32[]{:S(2)}, u32[]{:S(2)}) %collective-permute-start.35) | collective-permute-done | bytes 73760 | tf_op jit(solution)/shard_map/ppermute | solution.py:533
  (75 shorter events, 49.3 us)
Async XLA Ops:
  3.6 16.2 %collective-permute-start.7 = (bf16[128,1792]{1,0:T(8,128)(2,1)S(1)}, bf16[128,1792]{1,0:T(8,128)(2,1)S(1)}, u32[]{:S(2)}, u32[]{:S(2)}) collective-permute-start(bf16[128,1792]{1,0:T(8,128)(2,1)S(1)} %get-tuple-element.64.refs_0_), channel_id=1, source_target_pairs={{0,32},{1,225},{32,64},{33,1},{64,96},{65,33},{96,128},{97,65},{12... | collective-permute-start | bytes 1376264 | tf_op jit(solution)/shard_map/ppermute | solution.py:386
  5.6 17.3 %collective-permute-start.8 = (bf16[128,1792]{1,0:T(8,128)(2,1)S(1)}, bf16[128,1792]{1,0:T(8,128)(2,1)S(1)}, u32[]{:S(2)}, u32[]{:S(2)}) collective-permute-start(bf16[128,1792]{1,0:T(8,128)(2,1)S(1)} %get-tuple-element.64.refs_0_), channel_id=1, source_target_pairs={{0,64},{1,193},{32,96},{33,225},{64,128},{65,1},{96,160},{97,33},{... | collective-permute-start | bytes 1376264 | tf_op jit(solution)/shard_map/ppermute | solution.py:386
  8.9 7.2 %collective-permute-start.4 = (bf16[64,1792]{1,0:T(8,128)(2,1)S(1)}, bf16[64,1792]{1,0:T(8,128)(2,1)S(1)}, u32[]{:S(2)}, u32[]{:S(2)}) collective-permute-start(bf16[64,1792]{1,0:T(8,128)(2,1)S(1)} %get-tuple-element.65.a_ref), channel_id=1, source_target_pairs={{0,2},{1,5},{2,16},{3,7},{4,6},{5,9},{6,20},{7,11},{8,10},{9,13},{... | collective-permute-start | bytes 688136 | tf_op jit(solution)/shard_map/ppermute | solution.py:382
  12.1 7.7 %collective-permute-start.6 = (bf16[64,1792]{1,0:T(8,128)(2,1)S(1)}, bf16[64,1792]{1,0:T(8,128)(2,1)S(1)}, u32[]{:S(2)}, u32[]{:S(2)}) collective-permute-start(bf16[64,1792]{1,0:T(8,128)(2,1)S(1)} %get-tuple-element.65.a_ref), channel_id=1, source_target_pairs={{0,16},{1,9},{2,18},{3,11},{4,20},{5,13},{6,22},{7,15},{8,24},{9,1... | collective-permute-start | bytes 688136 | tf_op jit(solution)/shard_map/ppermute | solution.py:382
  23.0 13.5 %collective-permute-start.14 = (bf16[256,1792]{1,0:T(8,128)(2,1)S(1)}, bf16[256,1792]{1,0:T(8,128)(2,1)S(1)}, u32[]{:S(2)}, u32[]{:S(2)}) collective-permute-start(bf16[256,1792]{1,0:T(8,128)(2,1)S(1)} %column.1.refs_0_), channel_id=1, source_target_pairs={{0,4},{1,3},{2,6},{3,17},{4,8},{5,7},{6,10},{7,21},{8,12},{9,11},{... | collective-permute-start | bytes 2752520 | tf_op jit(solution)/shard_map/ppermute | solution.py:382
  24.6 7.2 %collective-permute-start.11 = (bf16[64,1792]{1,0:T(8,128)(2,1)S(1)}, bf16[64,1792]{1,0:T(8,128)(2,1)S(1)}, u32[]{:S(2)}, u32[]{:S(2)}) collective-permute-start(bf16[64,1792]{1,0:T(8,128)(2,1)S(1)} %get-tuple-element.124), channel_id=1, source_target_pairs={{0,1},{1,0},{2,3},{3,2},{4,5},{5,4},{6,7},{7,6},{8,9},{9,8},{10,11... | collective-permute-start | bytes 688136 | tf_op jit(solution)/shard_map/ppermute | solution.py:356
  26.4 12.4 %collective-permute-start.13 = (bf16[64,1792]{1,0:T(8,128)(2,1)S(1)}, bf16[64,1792]{1,0:T(8,128)(2,1)S(1)}, u32[]{:S(2)}, u32[]{:S(2)}) collective-permute-start(bf16[64,1792]{1,0:T(8,128)(2,1)S(1)} %get-tuple-element.123), channel_id=1, source_target_pairs={{0,64},{1,193},{32,96},{33,225},{64,128},{65,1},{96,160},{97,33},{... | collective-permute-start | bytes 688136 | tf_op jit(solution)/shard_map/ppermute | solution.py:386
  28.8 12.3 %collective-permute-start.9 = (bf16[128,1792]{1,0:T(8,128)(2,1)S(1)}, bf16[128,1792]{1,0:T(8,128)(2,1)S(1)}, u32[]{:S(2)}, u32[]{:S(2)}) collective-permute-start(bf16[128,1792]{1,0:T(8,128)(2,1)S(1)} %collective-permute-done.7.refs_1_), channel_id=1, source_target_pairs={{0,64},{1,193},{32,96},{33,225},{64,128},{65,1},{96,160},{97,33},{... | collective-permute-start | bytes 1376264 | tf_op jit(solution)/shard_map/ppermute | solution.py:386
  31.3 19.1 %collective-permute-start.18 = (bf16[256,1792]{1,0:T(8,128)(2,1)S(1)}, bf16[256,1792]{1,0:T(8,128)(2,1)S(1)}, u32[]{:S(2)}, u32[]{:S(2)}) collective-permute-start(bf16[256,1792]{1,0:T(8,128)(2,1)S(1)} %column.1.refs_0_), channel_id=1, source_target_pairs={{0,12},{1,19},{2,14},{3,1},{4,0},{5,23},{6,2},{7,5},{8,4},{9,27},{... | collective-permute-start | bytes 2752520 | tf_op jit(solution)/shard_map/ppermute | solution.py:382
  31.9 19.1 %collective-permute-start.16 = (bf16[256,1792]{1,0:T(8,128)(2,1)S(1)}, bf16[256,1792]{1,0:T(8,128)(2,1)S(1)}, u32[]{:S(2)}, u32[]{:S(2)}) collective-permute-start(bf16[256,1792]{1,0:T(8,128)(2,1)S(1)} %column.1.refs_0_), channel_id=1, source_target_pairs={{0,1},{1,0},{2,3},{3,2},{4,5},{5,4},{6,7},{7,6},{8,9},{9,8},{10,11... | collective-permute-start | bytes 2752520 | tf_op jit(solution)/shard_map/ppermute | solution.py:356
  36.5 17.6 %collective-permute-start.17 = (bf16[256,1792]{1,0:T(8,128)(2,1)S(1)}, bf16[256,1792]{1,0:T(8,128)(2,1)S(1)}, u32[]{:S(2)}, u32[]{:S(2)}) collective-permute-start(bf16[256,1792]{1,0:T(8,128)(2,1)S(1)} %collective-permute-done.14.refs_0_), channel_id=1, source_target_pairs={{0,1},{1,0},{2,3},{3,2},{4,5},{5,4},{6,7},{7,6},{8,9},{9,8},{10,11... | collective-permute-start | bytes 2752520 | tf_op jit(solution)/shard_map/ppermute | solution.py:356
  38.8 18.9 %collective-permute-start.15 = (bf16[256,1792]{1,0:T(8,128)(2,1)S(1)}, bf16[256,1792]{1,0:T(8,128)(2,1)S(1)}, u32[]{:S(2)}, u32[]{:S(2)}) collective-permute-start(bf16[256,1792]{1,0:T(8,128)(2,1)S(1)} %collective-permute-done.14.refs_0_), channel_id=1, source_target_pairs={{0,4},{1,3},{2,6},{3,17},{4,8},{5,7},{6,10},{7,21},{8,12},{9,11},{... | collective-permute-start | bytes 2752520 | tf_op jit(solution)/shard_map/ppermute | solution.py:382
  50.5 7.5 %collective-permute-start.19 = (bf16[256,1792]{1,0:T(8,128)(2,1)S(1)}, bf16[256,1792]{1,0:T(8,128)(2,1)S(1)}, u32[]{:S(2)}, u32[]{:S(2)}) collective-permute-start(bf16[256,1792]{1,0:T(8,128)(2,1)S(1)} %collective-permute-done.18.refs_0_), channel_id=1, source_target_pairs={{0,1},{1,0},{2,3},{3,2},{4,5},{5,4},{6,7},{7,6},{8,9},{9,8},{10,11... | collective-permute-start | bytes 2752520 | tf_op jit(solution)/shard_map/ppermute | solution.py:356
  66.2 8.0 %collective-permute-start.21 = (f32[8,512]{1,0:T(8,128)S(1)}, f32[8,512]{1,0:T(8,128)S(1)}, u32[]{:S(2)}, u32[]{:S(2)}) collective-permute-start(f32[8,512]{1,0:T(8,128)S(1)} %get-tuple-element.91.own_ref.flat_ref), channel_id=1, source_target_pairs={{0,224},{32,0},{64,32},{96,64},{128,96},{160,128},{192,160},{224,1... | collective-permute-start | bytes 49160 | tf_op jit(solution)/shard_map/ppermute | solution.py:465
  75.1 6.3 %collective-permute-start.23 = (f32[8,512]{1,0:T(8,128)S(1)}, f32[8,512]{1,0:T(8,128)S(1)}, u32[]{:S(2)}, u32[]{:S(2)}) collective-permute-start(f32[8,512]{1,0:T(8,128)S(1)} %get-tuple-element.99.window_ref), channel_id=1, source_target_pairs={{0,160},{32,192},{64,224},{96,0},{128,32},{160,64},{192,96},{224,1... | collective-permute-start | bytes 49160 | tf_op jit(solution)/shard_map/ppermute | solution.py:474
  78.1 6.8 %collective-permute-start.24 = (f32[8,512]{1,0:T(8,128)S(1)}, f32[8,512]{1,0:T(8,128)S(1)}, u32[]{:S(2)}, u32[]{:S(2)}) collective-permute-start(f32[8,512]{1,0:T(8,128)S(1)} %get-tuple-element.100), channel_id=1, source_target_pairs={{0,96},{32,128},{64,160},{96,192},{128,224},{160,0},{192,32},{224,... | collective-permute-start | bytes 49160 | tf_op jit(solution)/shard_map/ppermute | solution.py:475
  91.1 7.3 %collective-permute-start.26 = (bf16[112,768]{1,0:T(8,128)(2,1)S(1)}, bf16[112,768]{1,0:T(8,128)(2,1)S(1)}, u32[]{:S(2)}, u32[]{:S(2)}) collective-permute-start(bf16[112,768]{1,0:T(8,128)(2,1)S(1)} %get-tuple-element.115), channel_id=1, source_target_pairs={{0,4},{4,8},{8,12},{12,0},{1,5},{5,9},{9,13},{13,1},{2,6},{6,10},{... | collective-permute-start | bytes 516104 | tf_op jit(solution)/shard_map/ppermute | solution.py:508
  92.6 6.6 %collective-permute-start.27 = (bf16[112,768]{1,0:T(8,128)(2,1)S(1)}, bf16[112,768]{1,0:T(8,128)(2,1)S(1)}, u32[]{:S(2)}, u32[]{:S(2)}) collective-permute-start(bf16[112,768]{1,0:T(8,128)(2,1)S(1)} %get-tuple-element.116), channel_id=1, source_target_pairs={{0,12},{4,0},{8,4},{12,8},{1,13},{5,1},{9,5},{13,9},{2,14},{6,2},{... | collective-permute-start | bytes 516104 | tf_op jit(solution)/shard_map/ppermute | solution.py:508
  93.2 9.8 %collective-permute-start.28 = (bf16[112,768]{1,0:T(8,128)(2,1)S(1)}, bf16[112,768]{1,0:T(8,128)(2,1)S(1)}, u32[]{:S(2)}, u32[]{:S(2)}) collective-permute-start(bf16[112,768]{1,0:T(8,128)(2,1)S(1)} %get-tuple-element.117), channel_id=1, source_target_pairs={{0,8},{4,12},{8,0},{12,4},{1,9},{5,13},{9,1},{13,5},{2,10},{6,14},... | collective-permute-start | bytes 516104 | tf_op jit(solution)/shard_map/ppermute | solution.py:508
  103.7 9.4 %collective-permute-start.29 = (f32[56,768]{1,0:T(8,128)S(1)}, f32[56,768]{1,0:T(8,128)S(1)}, u32[]{:S(2)}, u32[]{:S(2)}) collective-permute-start(f32[56,768]{1,0:T(8,128)S(1)} %get-tuple-element.119), channel_id=1, source_target_pairs={{0,2},{2,16},{16,18},{18,0},{1,3},{3,17},{17,19},{19,1},{4,6},{6,2... | collective-permute-start | bytes 516104 | tf_op jit(solution)/shard_map/ppermute | solution.py:526
  105.3 7.8 %collective-permute-start.30 = (f32[56,768]{1,0:T(8,128)S(1)}, f32[56,768]{1,0:T(8,128)S(1)}, u32[]{:S(2)}, u32[]{:S(2)}) collective-permute-start(f32[56,768]{1,0:T(8,128)S(1)} %get-tuple-element.119), channel_id=1, source_target_pairs={{0,18},{2,0},{16,2},{18,16},{1,19},{3,1},{17,3},{19,17},{4,22},{6,... | collective-permute-start | bytes 516104 | tf_op jit(solution)/shard_map/ppermute | solution.py:526
  113.3 6.4 %collective-permute-start.33 = (f32[48,768]{1,0:T(8,128)S(1)}, f32[48,768]{1,0:T(8,128)S(1)}, u32[]{:S(2)}, u32[]{:S(2)}) collective-permute-start(f32[48,768]{1,0:T(8,128)S(1)} %get-tuple-element.122), channel_id=1, source_target_pairs={{0,32},{32,64},{64,96},{96,128},{128,160},{160,192},{192,224},{224... | collective-permute-start | bytes 442376 | tf_op jit(solution)/shard_map/ppermute | solution.py:528
  119.7 6.2 %collective-permute-start.34 = (bf16[48,768]{1,0:T(8,128)(2,1)S(1)}, bf16[48,768]{1,0:T(8,128)(2,1)S(1)}, u32[]{:S(2)}, u32[]{:S(2)}) collective-permute-start(bf16[48,768]{1,0:T(8,128)(2,1)S(1)} %get-tuple-element.125), channel_id=1, source_target_pairs={{0,160},{32,192},{64,224},{96,0},{128,32},{160,64},{192,96},{224,1... | collective-permute-start | bytes 221192 | tf_op jit(solution)/shard_map/ppermute | solution.py:532
  120.9 8.2 %collective-permute-start.35 = (bf16[48,768]{1,0:T(8,128)(2,1)S(1)}, bf16[48,768]{1,0:T(8,128)(2,1)S(1)}, u32[]{:S(2)}, u32[]{:S(2)}) collective-permute-start(bf16[48,768]{1,0:T(8,128)(2,1)S(1)} %get-tuple-element.126), channel_id=1, source_target_pairs={{0,96},{32,128},{64,160},{96,192},{128,224},{160,0},{192,32},{224,... | collective-permute-start | bytes 221192 | tf_op jit(solution)/shard_map/ppermute | solution.py:533
  (13 other events, 90.0 us)
where the time goes:
time: 131 us
  starting transfers between devices  55.3 us (42%)
  waiting for transfers between devices  40.7 us (31%)
  Pallas kernels  29.2 us (22%)
  between operations  2.65 us (2%)
  other arithmetic  1.9 us (1%)
    pallas_call x4, Pallas kernels, per_device(): pl.pallas_call(make_block(n, final, gain, [v.shape[0] for v in block]), i...  14.9 us
    ppermute x12, starting transfers between devices, per_device(): swap = lambda v: lax.ppermute(v, 'c', flip(cn, 1))  13.4 us
    ppermute x4, starting transfers between devices, climb(): return lax.ppermute(v, ('z', 'c'), pairs)  10.2 us
    ppermute x6, starting transfers between devices, plane(): return lax.ppermute(v, ('yh', 'x', 'yl', 'c'), pairs)  8.81 us
    ppermute x6, waiting for transfers between devices, plane(): return lax.ppermute(v, ('yh', 'x', 'yl', 'c'), pairs)  8.28 us
    ppermute x3, waiting for transfers between devices, per_device(): got = [lax.ppermute(v, 'x', ring(xn, k)) for k, v in zip((1, 3, 2), sends)]  7.8 us
    ppermute x1, waiting for transfers between devices, per_device(): lax.ppermute(across, Y, ring(yn, 2))  4.44 us
    ppermute x3, starting transfers between devices, per_device(): got = [lax.ppermute(v, 'x', ring(xn, k)) for k, v in zip((1, 3, 2), sends)]  4.09 us
  transfers between devices with their start and end apart: 36, of which 19 were waited for; matrix products, arithmetic and copies ran while one was open for 2% of the time, Pallas kernels for 15%

commit v1 on v0

--- a/solution.py
+++ b/solution.py
@@ -24,7 +24,7 @@
 FREE = pl.CostEstimate(flops=1, bytes_accessed=1, transcendentals=0)
 LANES = 128
 STEP = 8
-GROUP = 32
+GROUP = 128
 PART = 256
 
 
@@ -67,6 +67,14 @@
     return (txt / jnp.sqrt(jnp.sum(txt * txt, axis=1, keepdims=True) + eps_value)).astype(BF16)
 
 
+def onward_kernel(one_ref, two_ref, on_ref, across_ref):
+    rows = one_ref.shape[0] // 2
+    on_ref[:2 * rows, :] = one_ref[...]
+    on_ref[2 * rows:, :] = two_ref[:rows, :]
+    across_ref[:rows, :] = one_ref[rows:, :]
+    across_ref[rows:, :] = two_ref[rows:, :]
+
+
 def column_kernel(a_ref, b_ref, c_ref, d_ref, out_ref):
     rows = a_ref.shape[0]
     for n, ref in enumerate((a_ref, b_ref, c_ref, d_ref)):
@@ -74,23 +82,25 @@
 
 
 def images_kernel(zn, dt, place_ref, own_txt_ref, proj_ref, *refs):
-    count = zn // 2 - 1
-    img_ref, mine, theirs, last_ref = refs[0], refs[1:1 + count], refs[1 + count:1 + 2 * count], refs[1 + 2 * count]
-    timg_ref, feat_ref, simg_ref, simgb_ref, inv_ref, self_ref, diag_ref = refs[2 + 2 * count:]
+    img_ref, one_ref, two_ref, ahead_ref, near_ref, third_ref = refs[:6]
+    timg_ref, feat_ref, simg_ref, simgb_ref, inv_ref, self_ref, diag_ref = refs[6:]
     rows = img_ref.shape[0] // 2
     z = place_ref[0]
     side = 1 - 2 * place_ref[1]
 
-    def put(ref, shift):
+    def put(ref, k, shift):
         at = pl.ds(pl.multiple_of(lax.rem(z + shift + zn, zn) * rows, rows), rows)
-        timg_ref[at, :] = ref[:rows, :dt]
-        feat_ref[at, :] = ref[:rows, dt:]
-
-    put(img_ref, 0)
-    for k in range(count):
-        put(mine[k], -side * (k + 1))
-        put(theirs[k], side * (k + 1))
-    put(last_ref, zn // 2)
+        timg_ref[at, :] = ref[k * rows:(k + 1) * rows, :dt]
+        feat_ref[at, :] = ref[k * rows:(k + 1) * rows, dt:]
+
+    put(img_ref, 0, 0)
+    put(one_ref, 0, -side)
+    put(two_ref, 0, -2 * side)
+    put(ahead_ref, 0, -3 * side)
+    put(ahead_ref, 2, zn // 2)
+    put(near_ref, 0, side)
+    put(near_ref, 1, 2 * side)
+    put(third_ref, 0, 3 * side)
 
     def part(p, none):
         some = pl.ds(pl.multiple_of(p * PART, PART), PART)
@@ -134,16 +144,11 @@
         for ref, n in zip(texts, sizes):
             stu_ref[index * span + at:index * span + at + n, :] = ref[:, dt:]
             at += n
-        def part(p, none):
-            rows = pl.ds(pl.multiple_of(p * PART, PART), PART)
-            at = 0
-            for ref, n in zip(texts, sizes):
-                tl[rows, at:at + n] = lax.dot_general(timg_ref[rows, :], ref[:, :dt], NT, preferred_element_type=F32)
-                sl[rows, at:at + n] = lax.dot_general(simgb_ref[rows, :], ref[:, dt:], NT, preferred_element_type=F32)
-                at += n
-            return none
-
-        lax.fori_loop(0, images // PART, part, 0)
+        at = 0
+        for ref, n in zip(texts, sizes):
+            tl[:, at:at + n] = lax.dot_general(timg_ref[...], ref[:, :dt], NT, preferred_element_type=F32)
+            sl[:, at:at + n] = lax.dot_general(simgb_ref[...], ref[:, dt:], NT, preferred_element_type=F32)
+            at += n
 
         def body(k, none):
             for u in range(0, GROUP, 2 * STEP):
@@ -386,7 +391,8 @@
         return lax.ppermute(v, ("z", "c"), pairs)
 
     together = lax.optimization_barrier
-    left, right, far, one, two = together((plane(txts, 1, 0), plane(txts, -1, 0), plane(txts, 2, 0), climb(imgs, 1), climb(imgs, 2)))
+    left, right, far, one = together((plane(txts, 1, 0), plane(txts, -1, 0), plane(txts, 2, 0), climb(imgs, 1)))
+    two = climb(imgs, 2)
     own_col = pl.pallas_call(
         column_kernel,
         in_specs=[VMEM] * 4,
@@ -397,21 +403,29 @@
     )(txts, left, right, far)
     left_col, right_col = plane(own_col, 1, 1), plane(own_col, -1, 1)
     far_col = plane(left_col, 1, 1)
-    three = climb(one, 2)
-    four = climb(two[:rows], 2)
-    mine = [one, two, three]
-    theirs = [swap(v[rows:]) for v in mine]
+    onward, across = pl.pallas_call(
+        onward_kernel,
+        in_specs=[VMEM] * 2,
+        out_specs=[VMEM] * 2,
+        out_shape=[shape((3 * rows, dt + feat), BF16), shape((2 * rows, dt + feat), BF16)],
+        compiler_params=params(),
+        cost_estimate=FREE,
+        name="onward",
+    )(one, two)
+    ahead = climb(onward, 2)
+    near = swap(across)
+    third = swap(ahead[rows:2 * rows])
 
     timg, feats, simg, simgb, inv, self_col, diag = pl.pallas_call(
         functools.partial(images_kernel, zn, dt),
-        in_specs=[SMEM] + [VMEM] * (4 + 2 * len(mine)),
+        in_specs=[SMEM] + [VMEM] * 8,
         out_specs=[VMEM] * 7,
         out_shape=[shape((images, dt), BF16), shape((images, feat), BF16), shape((images, ds), F32), shape((images, ds), BF16),
                    shape((images, LANES), F32), shape((images, LANES), F32), shape((rows, ds), F32)],
         compiler_params=params(),
         cost_estimate=FREE,
         name="images",
-    )(place, st_own, proj, imgs, *mine, *theirs, four)
+    )(place, st_own, proj, imgs, one, two, ahead, near, third)
 
     blocks = [(own_col, swap(own_col)), (left_col, swap(left_col)), (right_col, swap(right_col)), None]
     span = column * cn

time: 131 us -> 128 us (0.977)
  starting transfers between devices: 55.3 us -> 46.5 us
  waiting for transfers between devices: 40.7 us -> 49.3 us
  Pallas kernels: 29.2 us -> 25.1 us
    ppermute x4 -> x3, waiting for transfers between devices: 3.83 us -> 17.1 us  [climb(): return lax.ppermute(v, ('z', 'c'), pairs)]
    ppermute x12 -> x11, starting transfers between devices: 13.4 us -> 6.46 us  [per_device(): swap = lambda v: lax.ppermute(v, 'c', flip(cn, 1))]
    ppermute x6, waiting for transfers between devices: 8.28 us -> 2.44 us  [plane(): return lax.ppermute(v, ('yh', 'x', 'yl', 'c'), pairs)]
    pallas_call x4, Pallas kernels: 14.9 us -> 10.8 us  [per_device(): pl.pallas_call(make_block(n, final, gain, [v.shape[0] for v in block]), i...]
    ppermute x1, waiting for transfers between devices: 3.14 us -> 0.66 us  [per_device(): behind = lax.ppermute(pair.astype(BF16), 'z', ring(zn, 3))]
    ppermute x1, starting transfers between devices: 3.95 us -> 6.38 us  [per_device(): above = lax.ppermute(flat, 'z', ring(zn, zn - 1))]
    ppermute x4 -> x3, starting transfers between devices: 10.2 us -> 7.74 us  [climb(): return lax.ppermute(v, ('z', 'c'), pairs)]
    ppermute x1, starting transfers between devices: 1.68 us -> 0.37 us  [per_device(): lax.ppermute(across, Y, ring(yn, 2))]
  transfers between devices with their start and end apart: 36 -> 34, of which waited for: 19 -> 16; matrix products, arithmetic and copies ran while one was open for 2% -> 2% of each run, Pallas kernels for 15% -> 14%
where the time goes in v1:
time: 128 us; the launch traced here: 127 us
  waiting for transfers between devices  49.3 us (39%)
  starting transfers between devices  46.5 us (36%)
  Pallas kernels  25.1 us (20%)
  between operations  2.64 us (2%)
  other arithmetic  1.9 us (1%)
    ppermute x3, waiting for transfers between devices, climb(): return lax.ppermute(v, ('z', 'c'), pairs)  17.1 us
    pallas_call x4, Pallas kernels, per_device(): pl.pallas_call(make_block(n, final, gain, [v.shape[0] for v in block]), i...  10.8 us
    ppermute x3, waiting for transfers between devices, per_device(): got = [lax.ppermute(v, 'x', ring(xn, k)) for k, v in zip((1, 3, 2), sends)]  7.8 us
    ppermute x3, starting transfers between devices, climb(): return lax.ppermute(v, ('z', 'c'), pairs)  7.74 us
    ppermute x6, starting transfers between devices, plane(): return lax.ppermute(v, ('yh', 'x', 'yl', 'c'), pairs)  7.55 us
    ppermute x11, starting transfers between devices, per_device(): swap = lambda v: lax.ppermute(v, 'c', flip(cn, 1))  6.46 us
    ppermute x1, starting transfers between devices, per_device(): above = lax.ppermute(flat, 'z', ring(zn, zn - 1))  6.38 us
    ppermute x1, waiting for transfers between devices, per_device(): lax.ppermute(across, Y, ring(yn, 2))  5.75 us
  transfers between devices with their start and end apart: 34, of which 16 were waited for; matrix products, arithmetic and copies ran while one was open for 2% of the time, Pallas kernels for 14%

profile of v1, /device:TPU:2, one launch (start us, length us, event | category | flops | bytes accessed | tf_op | source)
XLA Modules:
  0.0 126.6 jit_solution(5562868267447549617)
XLA Ops:
  10.8 3.3 %collective-permute-start.8 = (bf16[128,1792]{1,0:T(8,128)(2,1)S(1)}, bf16[128,1792]{1,0:T(8,128)(2,1)S(1)}, u32[]{:S(2)}, u32[]{:S(2)}) collective-permute-start(bf16[128,1792]{1,0:T(8,128)(2,1)S(1)} %get-tuple-element.65.refs_0_), channel_id=1, source_target_pairs={{0,64},{1,193},{32,96},{33,225},{64,128},{65,1},{96,160},{97,33},{... | collective-permute-start | bytes 1376264 | tf_op jit(solution)/shard_map/ppermute | solution.py:391
  14.1 2.4 %collective-permute-done.6.d_ref = bf16[64,1792]{1,0:T(8,128)(2,1)S(1)} collective-permute-done((bf16[64,1792]{1,0:T(8,128)(2,1)S(1)}, bf16[64,1792]{1,0:T(8,128)(2,1)S(1)}, u32[]{:S(2)}, u32[]{:S(2)}) %collective-permute-start.6) | collective-permute-done | bytes 229408 | tf_op jit(solution)/shard_map/ppermute | solution.py:387
  18.2 8.1 %collective-permute-done.8.two_ref.refs_2_ = bf16[128,1792]{1,0:T(8,128)(2,1)S(1)} collective-permute-done((bf16[128,1792]{1,0:T(8,128)(2,1)S(1)}, bf16[128,1792]{1,0:T(8,128)(2,1)S(1)}, u32[]{:S(2)}, u32[]{:S(2)}) %collective-permute-start.8) | collective-permute-done | bytes 458784 | tf_op jit(solution)/shard_map/ppermute | solution.py:391
  26.4 2.5 %collective-permute-start.9 = (bf16[192,1792]{1,0:T(8,128)(2,1)S(1)}, bf16[192,1792]{1,0:T(8,128)(2,1)S(1)}, u32[]{:S(2)}, u32[]{:S(2)}) collective-permute-start(bf16[192,1792]{1,0:T(8,128)(2,1)S(1)} %get-tuple-element.68), channel_id=1, source_target_pairs={{0,64},{1,193},{32,96},{33,225},{64,128},{65,1},{96,160},{97,33},{... | collective-permute-start | bytes 2064392 | tf_op jit(solution)/shard_map/ppermute | solution.py:391
  30.3 2.8 %collective-permute-start.15 = (bf16[256,1792]{1,0:T(8,128)(2,1)S(1)}, bf16[256,1792]{1,0:T(8,128)(2,1)S(1)}, u32[]{:S(2)}, u32[]{:S(2)}) collective-permute-start(bf16[256,1792]{1,0:T(8,128)(2,1)S(1)} %collective-permute-done.12.refs_0_), channel_id=1, source_target_pairs={{0,1},{1,0},{2,3},{3,2},{4,5},{5,4},{6,7},{7,6},{8,9},{9,8},{10,11... | collective-permute-start | bytes 2752520 | tf_op jit(solution)/shard_map/ppermute | solution.py:361
  33.2 9.0 %collective-permute-done.9.refs_3_ = bf16[192,1792]{1,0:T(8,128)(2,1)S(1)} collective-permute-done((bf16[192,1792]{1,0:T(8,128)(2,1)S(1)}, bf16[192,1792]{1,0:T(8,128)(2,1)S(1)}, u32[]{:S(2)}, u32[]{:S(2)}) %collective-permute-start.9) | collective-permute-done | bytes 688160 | tf_op jit(solution)/shard_map/ppermute | solution.py:391
  45.8 2.0 %images.1 = (bf16[512,1024]{1,0:T(8,128)(2,1)S(1)}, bf16[512,768]{1,0:T(8,128)(2,1)S(1)}, f32[512,768]{1,0:T(8,128)S(1)}, bf16[512,768]{1,0:T(8,128)(2,1)S(1)}, ...) custom-call(s32[4]{0:T(128)S(1)} %pad_add_fusion.place_ref, ...), custom_call_target="tpu_custom_call" | custom-call | flops 1 | bytes 1 | tf_op jit(solution)/shard_map/images/pallas_call | solution.py:419
  48.3 2.1 %block0.1 = (bf16[512,2048]{1,0:T(8,128)(2,1)S(1)}, bf16[512,2048]{1,0:T(8,128)(2,1)S(1)}, bf16[512,2048]{1,0:T(8,128)(2,1)S(1)}, bf16[2048,768]{1,0:T(8,128)(2,...) custom-call(bf16[512,1024]{1,0:T(8,128)(2,1)S(1)} %get-tuple-element.70.timg_ref, ...), custom_call_target="tpu_custom_call" | custom-call | flops 1 | bytes 1 | tf_op jit(solution)/shard_map/block0/pallas_call | solution.py:440
  50.4 2.6 %block1.1 = (bf16[512,2048]{1,0:T(8,128)(2,1)S(1)}, bf16[512,2048]{1,0:T(8,128)(2,1)S(1)}, bf16[512,2048]{1,0:T(8,128)(2,1)S(1)}, bf16[2048,768]{1,0:T(8,128)(2,...) custom-call(bf16[512,1024]{1,0:T(8,128)(2,1)S(1)} %get-tuple-element, ...), custom_call_target="tpu_custom_call", output_to_operand_aliasing={{0}: (5, {}), {1}: (6, {}), {2}: (7, {}), {3}: (8, {}), {4}... | custom-call | flops 1 | bytes 1 | tf_op jit(solution)/shard_map/block1/pallas_call | solution.py:440
  53.2 2.6 %block2.1 = (bf16[512,2048]{1,0:T(8,128)(2,1)S(1)}, bf16[512,2048]{1,0:T(8,128)(2,1)S(1)}, bf16[512,2048]{1,0:T(8,128)(2,1)S(1)}, bf16[2048,768]{1,0:T(8,128)(2,...) custom-call(bf16[512,1024]{1,0:T(8,128)(2,1)S(1)} %get-tuple-element, ...), custom_call_target="tpu_custom_call", output_to_operand_aliasing={{0}: (5, {}), {1}: (6, {}), {2}: (7, {}), {3}: (8, {}), {4}... | custom-call | flops 1 | bytes 1 | tf_op jit(solution)/shard_map/block2/pallas_call | solution.py:440
  55.9 3.5 %block3.1 = (bf16[512,2048]{1,0:T(8,128)(2,1)S(1)}, bf16[512,2048]{1,0:T(8,128)(2,1)S(1)}, bf16[512,2048]{1,0:T(8,128)(2,1)S(1)}, bf16[2048,768]{1,0:T(8,128)(2,...) custom-call(bf16[512,1024]{1,0:T(8,128)(2,1)S(1)} %get-tuple-element, ...), custom_call_target="tpu_custom_call", output_to_operand_aliasing={{0}: (5, {}), {1}: (6, {}), {2}: (7, {}), {3}: (8, {}), {4}... | custom-call | flops 1 | bytes 1 | tf_op jit(solution)/shard_map/block3/pallas_call | solution.py:440
  59.4 6.4 %collective-permute-start.19 = (f32[8,512]{1,0:T(8,128)S(1)}, f32[8,512]{1,0:T(8,128)S(1)}, u32[]{:S(2)}, u32[]{:S(2)}) collective-permute-start(f32[8,512]{1,0:T(8,128)S(1)} %get-tuple-element.93.own_ref.flat_ref), channel_id=1, source_target_pairs={{0,224},{32,0},{64,32},{96,64},{128,96},{160,128},{192,160},{224,1... | collective-permute-start | bytes 49160 | tf_op jit(solution)/shard_map/ppermute | solution.py:479
  65.8 4.1 %student.1 = (bf16[512,768]{1,0:T(8,128)(2,1)S(1)}, bf16[512,768]{1,0:T(8,128)(2,1)S(1)}, bf16[768,512]{1,0:T(8,128)(2,1)S(1)}, f32[8,128]{1,0:T(8,128)S(1)}) custom-call(bf16[512,2048]{1,0:T(8,128)(2,1)S(1)} %get-tuple-element.94.se_ref, bf16[512,2048]{1,0:T(8,128)(2,1)S(1)} %get-tuple-element.95.sig_ref, bf16[2048,768]{1,0:T(8,128)(2,1)S(1)} %get-tuple-element.96.stu_ref, ...), custom_call_target="tpu_custom_call" | custom-call | flops 1 | bytes 1 | tf_op jit(solution)/shard_map/student/pallas_call | solution.py:458
  70.7 4.1 %collective-permute-start.21 = (f32[8,512]{1,0:T(8,128)S(1)}, f32[8,512]{1,0:T(8,128)S(1)}, u32[]{:S(2)}, u32[]{:S(2)}) collective-permute-start(f32[8,512]{1,0:T(8,128)S(1)} %get-tuple-element.101.window_ref), channel_id=1, source_target_pairs={{0,160},{32,192},{64,224},{96,0},{128,32},{160,64},{192,96},{224,1... | collective-permute-start | bytes 49160 | tf_op jit(solution)/shard_map/ppermute | solution.py:488
  75.2 2.4 %teacher.1.b_ref = bf16[512,768]{1,0:T(8,128)(2,1)S(1)} custom-call(bf16[512,2048]{1,0:T(8,128)(2,1)S(1)} %get-tuple-element.104.te_ref, bf16[2048,768]{1,0:T(8,128)(2,1)S(1)} %get-tuple-element.96.stu_ref, f32[512,768]{1,0:T(8,128)S(1)} %get-tuple-element.97.simg_ref, f32[512,128]{1,0:T(8,128)S(1)} %get-tuple-element.98.inv_ref, ...), custom_call_target="tpu_custom_call" | custom-call | flops 1 | bytes 1 | tf_op jit(solution)/shard_map/teacher/pallas_call | solution.py:467
  77.6 4.0 %collective-permute-done.22.behind_ref = f32[8,512]{1,0:T(8,128)S(1)} collective-permute-done((f32[8,512]{1,0:T(8,128)S(1)}, f32[8,512]{1,0:T(8,128)S(1)}, u32[]{:S(2)}, u32[]{:S(2)}) %collective-permute-start.22) | collective-permute-done | bytes 16416 | tf_op jit(solution)/shard_map/ppermute | solution.py:489
  81.6 2.3 %away.1 = (f32[392,768]{1,0:T(8,128)S(1)}, bf16[512,768]{1,0:T(8,128)(2,1)S(1)}, bf16[512,768]{1,0:T(8,128)(2,1)S(1)}, f32[8,512]{1,0:T(8,128)S(1)}) custom-call(s32[4]{0:T(128)S(1)} %pad_add_fusion.place_ref, f32[8,512]{1,0:T(8,128)S(1)} %get-tuple-element.101.window_ref, f32[8,512]{1,0:T(8,128)S(1)} %collective-permute-done.21.ahead_ref, ...), custom_call_target="tpu_custom_call" | custom-call | flops 1 | bytes 1 | tf_op jit(solution)/shard_map/away/pallas_call | solution.py:491
  89.7 2.1 %collective-permute-start.26 = (bf16[112,768]{1,0:T(8,128)(2,1)S(1)}, bf16[112,768]{1,0:T(8,128)(2,1)S(1)}, u32[]{:S(2)}, u32[]{:S(2)}) collective-permute-start(bf16[112,768]{1,0:T(8,128)(2,1)S(1)} %get-tuple-element.119), channel_id=1, source_target_pairs={{0,8},{4,12},{8,0},{12,4},{1,9},{5,13},{9,1},{13,5},{2,10},{6,14},... | collective-permute-start | bytes 516104 | tf_op jit(solution)/shard_map/ppermute | solution.py:522
  91.8 2.9 %collective-permute-done.24.p_ref = bf16[112,768]{1,0:T(8,128)(2,1)S(1)} collective-permute-done((bf16[112,768]{1,0:T(8,128)(2,1)S(1)}, bf16[112,768]{1,0:T(8,128)(2,1)S(1)}, u32[]{:S(2)}, u32[]{:S(2)}) %collective-permute-start.24) | collective-permute-done | bytes 172064 | tf_op jit(solution)/shard_map/ppermute | solution.py:522
  95.8 3.8 %collective-permute-done.26.r_ref = bf16[112,768]{1,0:T(8,128)(2,1)S(1)} collective-permute-done((bf16[112,768]{1,0:T(8,128)(2,1)S(1)}, bf16[112,768]{1,0:T(8,128)(2,1)S(1)}, u32[]{:S(2)}, u32[]{:S(2)}) %collective-permute-start.26) | collective-permute-done | bytes 172064 | tf_op jit(solution)/shard_map/ppermute | solution.py:522
  104.0 5.7 %collective-permute-done.29.r_ref = bf16[64,768]{1,0:T(8,128)(2,1)S(1)} collective-permute-done((bf16[64,768]{1,0:T(8,128)(2,1)S(1)}, bf16[64,768]{1,0:T(8,128)(2,1)S(1)}, u32[]{:S(2)}, u32[]{:S(2)}) %collective-permute-start.29) | collective-permute-done | bytes 98336 | tf_op jit(solution)/shard_map/ppermute | solution.py:540
  111.9 3.1 %collective-permute-done.30 = f32[48,768]{1,0:T(8,128)S(1)} collective-permute-done((f32[48,768]{1,0:T(8,128)S(1)}, f32[48,768]{1,0:T(8,128)S(1)}, u32[]{:S(2)}, u32[]{:S(2)}) %collective-permute-start.30) | collective-permute-done | bytes 147488 | tf_op jit(solution)/shard_map/ppermute | solution.py:543
  115.0 2.0 %collective-permute-done.31 = f32[48,768]{1,0:T(8,128)S(1)} collective-permute-done((f32[48,768]{1,0:T(8,128)S(1)}, f32[48,768]{1,0:T(8,128)S(1)}, u32[]{:S(2)}, u32[]{:S(2)}) %collective-permute-start.31) | collective-permute-done | bytes 147488 | tf_op jit(solution)/shard_map/ppermute | solution.py:542
  117.4 3.5 %collective-permute-start.33 = (bf16[48,768]{1,0:T(8,128)(2,1)S(1)}, bf16[48,768]{1,0:T(8,128)(2,1)S(1)}, u32[]{:S(2)}, u32[]{:S(2)}) collective-permute-start(bf16[48,768]{1,0:T(8,128)(2,1)S(1)} %get-tuple-element.126), channel_id=1, source_target_pairs={{0,96},{32,128},{64,160},{96,192},{128,224},{160,0},{192,32},{224,... | collective-permute-start | bytes 221192 | tf_op jit(solution)/shard_map/ppermute | solution.py:547
  (70 shorter events, 36.7 us)
Async XLA Ops:
  3.6 12.9 %collective-permute-start.7 = (bf16[128,1792]{1,0:T(8,128)(2,1)S(1)}, bf16[128,1792]{1,0:T(8,128)(2,1)S(1)}, u32[]{:S(2)}, u32[]{:S(2)}) collective-permute-start(bf16[128,1792]{1,0:T(8,128)(2,1)S(1)} %get-tuple-element.65.refs_0_), channel_id=1, source_target_pairs={{0,32},{1,225},{32,64},{33,1},{64,96},{65,33},{96,128},{97,65},{12... | collective-permute-start | bytes 1376264 | tf_op jit(solution)/shard_map/ppermute | solution.py:391
  5.6 8.5 %collective-permute-start.4 = (bf16[64,1792]{1,0:T(8,128)(2,1)S(1)}, bf16[64,1792]{1,0:T(8,128)(2,1)S(1)}, u32[]{:S(2)}, u32[]{:S(2)}) collective-permute-start(bf16[64,1792]{1,0:T(8,128)(2,1)S(1)} %get-tuple-element.66.a_ref), channel_id=1, source_target_pairs={{0,2},{1,5},{2,16},{3,7},{4,6},{5,9},{6,20},{7,11},{8,10},{9,13},{... | collective-permute-start | bytes 688136 | tf_op jit(solution)/shard_map/ppermute | solution.py:387
  7.2 6.9 %collective-permute-start.5 = (bf16[64,1792]{1,0:T(8,128)(2,1)S(1)}, bf16[64,1792]{1,0:T(8,128)(2,1)S(1)}, u32[]{:S(2)}, u32[]{:S(2)}) collective-permute-start(bf16[64,1792]{1,0:T(8,128)(2,1)S(1)} %get-tuple-element.66.a_ref), channel_id=1, source_target_pairs={{0,18},{1,13},{2,0},{3,15},{4,22},{5,1},{6,4},{7,3},{8,26},{9,5},{... | collective-permute-start | bytes 688136 | tf_op jit(solution)/shard_map/ppermute | solution.py:387
  8.9 7.7 %collective-permute-start.6 = (bf16[64,1792]{1,0:T(8,128)(2,1)S(1)}, bf16[64,1792]{1,0:T(8,128)(2,1)S(1)}, u32[]{:S(2)}, u32[]{:S(2)}) collective-permute-start(bf16[64,1792]{1,0:T(8,128)(2,1)S(1)} %get-tuple-element.66.a_ref), channel_id=1, source_target_pairs={{0,16},{1,9},{2,18},{3,11},{4,20},{5,13},{6,22},{7,15},{8,24},{9,1... | collective-permute-start | bytes 688136 | tf_op jit(solution)/shard_map/ppermute | solution.py:387
  10.8 15.4 %collective-permute-start.8 = (bf16[128,1792]{1,0:T(8,128)(2,1)S(1)}, bf16[128,1792]{1,0:T(8,128)(2,1)S(1)}, u32[]{:S(2)}, u32[]{:S(2)}) collective-permute-start(bf16[128,1792]{1,0:T(8,128)(2,1)S(1)} %get-tuple-element.65.refs_0_), channel_id=1, source_target_pairs={{0,64},{1,193},{32,96},{33,225},{64,128},{65,1},{96,160},{97,33},{... | collective-permute-start | bytes 1376264 | tf_op jit(solution)/shard_map/ppermute | solution.py:391
  16.6 13.6 %collective-permute-start.12 = (bf16[256,1792]{1,0:T(8,128)(2,1)S(1)}, bf16[256,1792]{1,0:T(8,128)(2,1)S(1)}, u32[]{:S(2)}, u32[]{:S(2)}) collective-permute-start(bf16[256,1792]{1,0:T(8,128)(2,1)S(1)} %column.1.refs_0_), channel_id=1, source_target_pairs={{0,4},{1,3},{2,6},{3,17},{4,8},{5,7},{6,10},{7,21},{8,12},{9,11},{... | collective-permute-start | bytes 2752520 | tf_op jit(solution)/shard_map/ppermute | solution.py:387
  26.4 15.9 %collective-permute-start.9 = (bf16[192,1792]{1,0:T(8,128)(2,1)S(1)}, bf16[192,1792]{1,0:T(8,128)(2,1)S(1)}, u32[]{:S(2)}, u32[]{:S(2)}) collective-permute-start(bf16[192,1792]{1,0:T(8,128)(2,1)S(1)} %get-tuple-element.68), channel_id=1, source_target_pairs={{0,64},{1,193},{32,96},{33,225},{64,128},{65,1},{96,160},{97,33},{... | collective-permute-start | bytes 2064392 | tf_op jit(solution)/shard_map/ppermute | solution.py:391
  28.8 19.0 %collective-permute-start.16 = (bf16[256,1792]{1,0:T(8,128)(2,1)S(1)}, bf16[256,1792]{1,0:T(8,128)(2,1)S(1)}, u32[]{:S(2)}, u32[]{:S(2)}) collective-permute-start(bf16[256,1792]{1,0:T(8,128)(2,1)S(1)} %column.1.refs_0_), channel_id=1, source_target_pairs={{0,12},{1,19},{2,14},{3,1},{4,0},{5,23},{6,2},{7,5},{8,4},{9,27},{... | collective-permute-start | bytes 2752520 | tf_op jit(solution)/shard_map/ppermute | solution.py:387
  29.4 18.9 %collective-permute-start.14 = (bf16[256,1792]{1,0:T(8,128)(2,1)S(1)}, bf16[256,1792]{1,0:T(8,128)(2,1)S(1)}, u32[]{:S(2)}, u32[]{:S(2)}) collective-permute-start(bf16[256,1792]{1,0:T(8,128)(2,1)S(1)} %column.1.refs_0_), channel_id=1, source_target_pairs={{0,1},{1,0},{2,3},{3,2},{4,5},{5,4},{6,7},{7,6},{8,9},{9,8},{10,11... | collective-permute-start | bytes 2752520 | tf_op jit(solution)/shard_map/ppermute | solution.py:361
  30.3 20.2 %collective-permute-start.15 = (bf16[256,1792]{1,0:T(8,128)(2,1)S(1)}, bf16[256,1792]{1,0:T(8,128)(2,1)S(1)}, u32[]{:S(2)}, u32[]{:S(2)}) collective-permute-start(bf16[256,1792]{1,0:T(8,128)(2,1)S(1)} %collective-permute-done.12.refs_0_), channel_id=1, source_target_pairs={{0,1},{1,0},{2,3},{3,2},{4,5},{5,4},{6,7},{7,6},{8,9},{9,8},{10,11... | collective-permute-start | bytes 2752520 | tf_op jit(solution)/shard_map/ppermute | solution.py:361
  33.0 20.0 %collective-permute-start.13 = (bf16[256,1792]{1,0:T(8,128)(2,1)S(1)}, bf16[256,1792]{1,0:T(8,128)(2,1)S(1)}, u32[]{:S(2)}, u32[]{:S(2)}) collective-permute-start(bf16[256,1792]{1,0:T(8,128)(2,1)S(1)} %collective-permute-done.12.refs_0_), channel_id=1, source_target_pairs={{0,4},{1,3},{2,6},{3,17},{4,8},{5,7},{6,10},{7,21},{8,12},{9,11},{... | collective-permute-start | bytes 2752520 | tf_op jit(solution)/shard_map/ppermute | solution.py:387
  47.8 5.4 %collective-permute-start.17 = (bf16[256,1792]{1,0:T(8,128)(2,1)S(1)}, bf16[256,1792]{1,0:T(8,128)(2,1)S(1)}, u32[]{:S(2)}, u32[]{:S(2)}) collective-permute-start(bf16[256,1792]{1,0:T(8,128)(2,1)S(1)} %collective-permute-done.16.refs_0_), channel_id=1, source_target_pairs={{0,1},{1,0},{2,3},{3,2},{4,5},{5,4},{6,7},{7,6},{8,9},{9,8},{10,11... | collective-permute-start | bytes 2752520 | tf_op jit(solution)/shard_map/ppermute | solution.py:361
  59.4 10.5 %collective-permute-start.19 = (f32[8,512]{1,0:T(8,128)S(1)}, f32[8,512]{1,0:T(8,128)S(1)}, u32[]{:S(2)}, u32[]{:S(2)}) collective-permute-start(f32[8,512]{1,0:T(8,128)S(1)} %get-tuple-element.93.own_ref.flat_ref), channel_id=1, source_target_pairs={{0,224},{32,0},{64,32},{96,64},{128,96},{160,128},{192,160},{224,1... | collective-permute-start | bytes 49160 | tf_op jit(solution)/shard_map/ppermute | solution.py:479
  70.7 6.9 %collective-permute-start.21 = (f32[8,512]{1,0:T(8,128)S(1)}, f32[8,512]{1,0:T(8,128)S(1)}, u32[]{:S(2)}, u32[]{:S(2)}) collective-permute-start(f32[8,512]{1,0:T(8,128)S(1)} %get-tuple-element.101.window_ref), channel_id=1, source_target_pairs={{0,160},{32,192},{64,224},{96,0},{128,32},{160,64},{192,96},{224,1... | collective-permute-start | bytes 49160 | tf_op jit(solution)/shard_map/ppermute | solution.py:488
  74.8 6.7 %collective-permute-start.22 = (f32[8,512]{1,0:T(8,128)S(1)}, f32[8,512]{1,0:T(8,128)S(1)}, u32[]{:S(2)}, u32[]{:S(2)}) collective-permute-start(f32[8,512]{1,0:T(8,128)S(1)} %get-tuple-element.102), channel_id=1, source_target_pairs={{0,96},{32,128},{64,160},{96,192},{128,224},{160,0},{192,32},{224,... | collective-permute-start | bytes 49160 | tf_op jit(solution)/shard_map/ppermute | solution.py:489
  87.6 7.1 %collective-permute-start.24 = (bf16[112,768]{1,0:T(8,128)(2,1)S(1)}, bf16[112,768]{1,0:T(8,128)(2,1)S(1)}, u32[]{:S(2)}, u32[]{:S(2)}) collective-permute-start(bf16[112,768]{1,0:T(8,128)(2,1)S(1)} %get-tuple-element.117), channel_id=1, source_target_pairs={{0,4},{4,8},{8,12},{12,0},{1,5},{5,9},{9,13},{13,1},{2,6},{6,10},{... | collective-permute-start | bytes 516104 | tf_op jit(solution)/shard_map/ppermute | solution.py:522
  89.2 6.6 %collective-permute-start.25 = (bf16[112,768]{1,0:T(8,128)(2,1)S(1)}, bf16[112,768]{1,0:T(8,128)(2,1)S(1)}, u32[]{:S(2)}, u32[]{:S(2)}) collective-permute-start(bf16[112,768]{1,0:T(8,128)(2,1)S(1)} %get-tuple-element.118), channel_id=1, source_target_pairs={{0,12},{4,0},{8,4},{12,8},{1,13},{5,1},{9,5},{13,9},{2,14},{6,2},{... | collective-permute-start | bytes 516104 | tf_op jit(solution)/shard_map/ppermute | solution.py:522
  89.7 9.9 %collective-permute-start.26 = (bf16[112,768]{1,0:T(8,128)(2,1)S(1)}, bf16[112,768]{1,0:T(8,128)(2,1)S(1)}, u32[]{:S(2)}, u32[]{:S(2)}) collective-permute-start(bf16[112,768]{1,0:T(8,128)(2,1)S(1)} %get-tuple-element.119), channel_id=1, source_target_pairs={{0,8},{4,12},{8,0},{12,4},{1,9},{5,13},{9,1},{13,5},{2,10},{6,14},... | collective-permute-start | bytes 516104 | tf_op jit(solution)/shard_map/ppermute | solution.py:522
  100.3 9.4 %collective-permute-start.27 = (f32[56,768]{1,0:T(8,128)S(1)}, f32[56,768]{1,0:T(8,128)S(1)}, u32[]{:S(2)}, u32[]{:S(2)}) collective-permute-start(f32[56,768]{1,0:T(8,128)S(1)} %get-tuple-element.121), channel_id=1, source_target_pairs={{0,2},{2,16},{16,18},{18,0},{1,3},{3,17},{17,19},{19,1},{4,6},{6,2... | collective-permute-start | bytes 516104 | tf_op jit(solution)/shard_map/ppermute | solution.py:540
  101.8 7.9 %collective-permute-start.28 = (f32[56,768]{1,0:T(8,128)S(1)}, f32[56,768]{1,0:T(8,128)S(1)}, u32[]{:S(2)}, u32[]{:S(2)}) collective-permute-start(f32[56,768]{1,0:T(8,128)S(1)} %get-tuple-element.121), channel_id=1, source_target_pairs={{0,18},{2,0},{16,2},{18,16},{1,19},{3,1},{17,3},{19,17},{4,22},{6,... | collective-permute-start | bytes 516104 | tf_op jit(solution)/shard_map/ppermute | solution.py:540
  103.6 6.1 %collective-permute-start.29 = (bf16[64,768]{1,0:T(8,128)(2,1)S(1)}, bf16[64,768]{1,0:T(8,128)(2,1)S(1)}, u32[]{:S(2)}, u32[]{:S(2)}) collective-permute-start(bf16[64,768]{1,0:T(8,128)(2,1)S(1)} %get-tuple-element.122), channel_id=1, source_target_pairs={{0,16},{2,18},{16,0},{18,2},{1,17},{3,19},{17,1},{19,3},{4,20},{6,... | collective-permute-start | bytes 294920 | tf_op jit(solution)/shard_map/ppermute | solution.py:540
  110.6 6.4 %collective-permute-start.31 = (f32[48,768]{1,0:T(8,128)S(1)}, f32[48,768]{1,0:T(8,128)S(1)}, u32[]{:S(2)}, u32[]{:S(2)}) collective-permute-start(f32[48,768]{1,0:T(8,128)S(1)} %get-tuple-element.124), channel_id=1, source_target_pairs={{0,32},{32,64},{64,96},{96,128},{128,160},{160,192},{192,224},{224... | collective-permute-start | bytes 442376 | tf_op jit(solution)/shard_map/ppermute | solution.py:542
  117.0 7.1 %collective-permute-start.32 = (bf16[48,768]{1,0:T(8,128)(2,1)S(1)}, bf16[48,768]{1,0:T(8,128)(2,1)S(1)}, u32[]{:S(2)}, u32[]{:S(2)}) collective-permute-start(bf16[48,768]{1,0:T(8,128)(2,1)S(1)} %get-tuple-element.125), channel_id=1, source_target_pairs={{0,160},{32,192},{64,224},{96,0},{128,32},{160,64},{192,96},{224,1... | collective-permute-start | bytes 221192 | tf_op jit(solution)/shard_map/ppermute | solution.py:546
  117.4 7.4 %collective-permute-start.33 = (bf16[48,768]{1,0:T(8,128)(2,1)S(1)}, bf16[48,768]{1,0:T(8,128)(2,1)S(1)}, u32[]{:S(2)}, u32[]{:S(2)}) collective-permute-start(bf16[48,768]{1,0:T(8,128)(2,1)S(1)} %get-tuple-element.126), channel_id=1, source_target_pairs={{0,96},{32,128},{64,160},{96,192},{128,224},{160,0},{192,32},{224,... | collective-permute-start | bytes 221192 | tf_op jit(solution)/shard_map/ppermute | solution.py:547
  (11 other events, 70.3 us)

commit v2 on v1

--- a/solution.py
+++ b/solution.py
@@ -81,47 +81,50 @@
         out_ref[n * rows:(n + 1) * rows, :] = ref[...]
 
 
-def images_kernel(zn, dt, place_ref, own_txt_ref, proj_ref, *refs):
-    img_ref, one_ref, two_ref, ahead_ref, near_ref, third_ref = refs[:6]
-    timg_ref, feat_ref, simg_ref, simgb_ref, inv_ref, self_ref, diag_ref = refs[6:]
-    rows = img_ref.shape[0] // 2
-    z = place_ref[0]
+def ring_rows(place_ref, zn, rows, shift):
     side = 1 - 2 * place_ref[1]
-
-    def put(ref, k, shift):
-        at = pl.ds(pl.multiple_of(lax.rem(z + shift + zn, zn) * rows, rows), rows)
-        timg_ref[at, :] = ref[k * rows:(k + 1) * rows, :dt]
-        feat_ref[at, :] = ref[k * rows:(k + 1) * rows, dt:]
-
-    put(img_ref, 0, 0)
-    put(one_ref, 0, -side)
-    put(two_ref, 0, -2 * side)
-    put(ahead_ref, 0, -3 * side)
-    put(ahead_ref, 2, zn // 2)
-    put(near_ref, 0, side)
-    put(near_ref, 1, 2 * side)
-    put(third_ref, 0, 3 * side)
-
-    def part(p, none):
-        some = pl.ds(pl.multiple_of(p * PART, PART), PART)
-        pre = jnp.dot(feat_ref[some, :], proj_ref[...], preferred_element_type=F32)
-        norm = jnp.sqrt(jnp.sum(pre * pre, axis=1, keepdims=True) + eps_value)
-        simg = pre / norm
-        simg_ref[some, :] = simg
-        simgb_ref[some, :] = simg.astype(BF16)
-        inv_ref[some, :] = jnp.broadcast_to(1.0 / norm, (PART, LANES))
-        return none
-
-    lax.fori_loop(0, simg_ref.shape[0] // PART, part, 0)
-    own = pl.ds(pl.multiple_of(z * rows, rows), rows)
-    s = simg_ref[own, :]
+    return pl.ds(pl.multiple_of(lax.rem(place_ref[0] + side * shift + zn, zn) * rows, rows), rows)
+
+
+def embed(zn, dt, place_ref, proj_ref, pieces, shifts, outs, feats):
+    timg_ref, feat_ref, simg_ref, simgb_ref, inv_ref = outs
+    rows = feats.shape[0] // len(pieces)
+    for k, ((ref, n), shift) in enumerate(zip(pieces, shifts)):
+        at = ring_rows(place_ref, zn, rows, shift)
+        timg_ref[at, :] = ref[n * rows:(n + 1) * rows, :dt]
+        feats[k * rows:(k + 1) * rows, :] = ref[n * rows:(n + 1) * rows, dt:]
+        feat_ref[at, :] = feats[k * rows:(k + 1) * rows, :]
+    pre = jnp.dot(feats[...], proj_ref[...], preferred_element_type=F32)
+    norm = jnp.sqrt(jnp.sum(pre * pre, axis=1, keepdims=True) + eps_value)
+    simg = pre / norm
+    inv = jnp.broadcast_to(1.0 / norm, (feats.shape[0], LANES))
+    for k, shift in enumerate(shifts):
+        at = ring_rows(place_ref, zn, rows, shift)
+        part = slice(k * rows, (k + 1) * rows)
+        simg_ref[at, :] = simg[part, :]
+        simgb_ref[at, :] = simg[part, :].astype(BF16)
+        inv_ref[at, :] = inv[part, :]
+    return rows
+
+
+def early_kernel(zn, dt, place_ref, proj_ref, own_txt_ref, img_ref, one_ref, two_ref, near_ref, *refs):
+    outs, (self_ref, diag_ref, done_ref, feats) = refs[:5], refs[5:]
+    pieces = [(img_ref, 0), (one_ref, 0), (two_ref, 0), (near_ref, 0), (near_ref, 1)]
+    rows = embed(zn, dt, place_ref, proj_ref, pieces, (0, -1, -2, 1, 2), outs, feats)
+    done_ref[...] = jnp.zeros_like(done_ref)
+    own = ring_rows(place_ref, zn, rows, 0)
+    s = outs[2][own, :]
     txt = own_txt_ref[...].astype(F32)
     margin = sig_scale * jnp.sum(s.astype(BF16).astype(F32) * txt, axis=1, keepdims=True) + sig_bias
     self_ref[...] = jnp.zeros_like(self_ref)
     lane = lax.broadcasted_iota(jnp.int32, (rows, LANES), 1)
     self_ref[own, :] = jnp.where(lane == 0, -margin, 0.0)
     d = -sig_scale * txt
-    diag_ref[...] = (d - s * jnp.sum(s * d, axis=1, keepdims=True)) * inv_ref[own, 0:1]
+    diag_ref[...] = (d - s * jnp.sum(s * d, axis=1, keepdims=True)) * outs[4][own, 0:1]
+
+
+def late_kernel(zn, dt, place_ref, proj_ref, ahead_ref, third_ref, *refs):
+    embed(zn, dt, place_ref, proj_ref, [(ahead_ref, 0), (third_ref, 0), (ahead_ref, 2)], (-3, 3, zn // 2), refs[6:11], refs[11])
 
 
 def make_block(index, last, gain, sizes):
@@ -402,7 +405,6 @@
         name="column",
     )(txts, left, right, far)
     left_col, right_col = plane(own_col, 1, 1), plane(own_col, -1, 1)
-    far_col = plane(left_col, 1, 1)
     onward, across = pl.pallas_call(
         onward_kernel,
         in_specs=[VMEM] * 2,
@@ -414,18 +416,31 @@
     )(one, two)
     ahead = climb(onward, 2)
     near = swap(across)
+    arrays = [shape((images, dt), BF16), shape((images, feat), BF16), shape((images, ds), F32), shape((images, ds), BF16), shape((images, LANES), F32)]
+    *arrays_early, self_col, diag, done_early = pl.pallas_call(
+        functools.partial(early_kernel, zn, dt),
+        in_specs=[SMEM] + [VMEM] * 6,
+        out_specs=[VMEM] * 8,
+        out_shape=arrays + [shape((images, LANES), F32), shape((rows, ds), F32), shape((8, LANES), F32)],
+        scratch_shapes=[pltpu.VMEM((5 * rows, feat), BF16)],
+        compiler_params=params(),
+        cost_estimate=FREE,
+        name="early",
+    )(place, proj, st_own, imgs, one, two, near)
+    left_col, done_early = together((left_col, done_early))
+    far_col = plane(left_col, 1, 1)
     third = swap(ahead[rows:2 * rows])
-
-    timg, feats, simg, simgb, inv, self_col, diag = pl.pallas_call(
-        functools.partial(images_kernel, zn, dt),
-        in_specs=[SMEM] + [VMEM] * 8,
-        out_specs=[VMEM] * 7,
-        out_shape=[shape((images, dt), BF16), shape((images, feat), BF16), shape((images, ds), F32), shape((images, ds), BF16),
-                   shape((images, LANES), F32), shape((images, LANES), F32), shape((rows, ds), F32)],
-        compiler_params=params(),
-        cost_estimate=FREE,
-        name="images",
-    )(place, st_own, proj, imgs, one, two, ahead, near, third)
+    timg, feats, simg, simgb, inv = pl.pallas_call(
+        functools.partial(late_kernel, zn, dt),
+        in_specs=[SMEM] + [VMEM] * 9,
+        out_specs=[VMEM] * 5,
+        out_shape=arrays,
+        scratch_shapes=[pltpu.VMEM((3 * rows, feat), BF16)],
+        input_output_aliases={4 + k: k for k in range(5)},
+        compiler_params=params(),
+        cost_estimate=FREE,
+        name="late",
+    )(place, proj, ahead, third, *arrays_early, done_early)
 
     blocks = [(own_col, swap(own_col)), (left_col, swap(left_col)), (right_col, swap(right_col)), None]
     span = column * cn

time: 128 us -> 127 us (level)
  waiting for transfers between devices: 49.3 us -> 46.9 us
    ppermute x1, starting transfers between devices: 6.38 us -> 2.99 us  [per_device(): above = lax.ppermute(flat, 'z', ring(zn, zn - 1))]
    ppermute x6, starting transfers between devices: 7.55 us -> 9.41 us  [plane(): return lax.ppermute(v, ('yh', 'x', 'yl', 'c'), pairs)]
    ppermute x11, waiting for transfers between devices: 4.11 us -> 2.58 us  [per_device(): swap = lambda v: lax.ppermute(v, 'c', flip(cn, 1))]
    ppermute x11, starting transfers between devices: 6.46 us -> 7.89 us  [per_device(): swap = lambda v: lax.ppermute(v, 'c', flip(cn, 1))]
    pallas_call x1 -> x2, Pallas kernels: 2.02 us -> 2.62 us  [the longest x1 1.51 us: per_device(): pl.pallas_call(functools.partial(early_kernel, zn, dt), in_specs=[SMEM] +...]
  transfers between devices with their start and end apart: 34 -> 34, of which waited for: 16 -> 14; matrix products, arithmetic and copies ran while one was open for 2% -> 2% of each run, Pallas kernels for 14% -> 14%
where the time goes in v2:
time: 127 us; the launch traced here: 125 us
  starting transfers between devices  47 us (37%)
  waiting for transfers between devices  46.9 us (37%)
  Pallas kernels  25.8 us (20%)
  between operations  2.65 us (2%)
  other arithmetic  1.9 us (1%)
    ppermute x3, waiting for transfers between devices, climb(): return lax.ppermute(v, ('z', 'c'), pairs)  16 us
    pallas_call x4, Pallas kernels, per_device(): pl.pallas_call(make_block(n, final, gain, [v.shape[0] for v in block]), i...  10.8 us
    ppermute x6, starting transfers between devices, plane(): return lax.ppermute(v, ('yh', 'x', 'yl', 'c'), pairs)  9.41 us
    ppermute x3, waiting for transfers between devices, per_device(): got = [lax.ppermute(v, 'x', ring(xn, k)) for k, v in zip((1, 3, 2), sends)]  8.08 us
    ppermute x11, starting transfers between devices, per_device(): swap = lambda v: lax.ppermute(v, 'c', flip(cn, 1))  7.89 us
    ppermute x3, starting transfers between devices, climb(): return lax.ppermute(v, ('z', 'c'), pairs)  7.66 us
    ppermute x1, waiting for transfers between devices, per_device(): lax.ppermute(across, Y, ring(yn, 2))  5.76 us
    ppermute x3, starting transfers between devices, per_device(): got = [lax.ppermute(v, 'x', ring(xn, k)) for k, v in zip((1, 3, 2), sends)]  4.91 us
  transfers between devices with their start and end apart: 34, of which 14 were waited for; matrix products, arithmetic and copies ran while one was open for 2% of the time, Pallas kernels for 14%

profile of v2, /device:TPU:2, one launch (start us, length us, event | category | flops | bytes accessed | tf_op | source)
XLA Modules:
  0.0 125.4 jit_solution(14751476892990015306)
XLA Ops:
  3.6 2.0 %collective-permute-start.7 = (bf16[128,1792]{1,0:T(8,128)(2,1)S(1)}, bf16[128,1792]{1,0:T(8,128)(2,1)S(1)}, u32[]{:S(2)}, u32[]{:S(2)}) collective-permute-start(bf16[128,1792]{1,0:T(8,128)(2,1)S(1)} %get-tuple-element.73.img_ref), channel_id=1, source_target_pairs={{0,32},{1,225},{32,64},{33,1},{64,96},{65,33},{96,128},{97,65},{12... | collective-permute-start | bytes 1376264 | tf_op jit(solution)/shard_map/ppermute | solution.py:394
  10.8 3.3 %collective-permute-start.8 = (bf16[128,1792]{1,0:T(8,128)(2,1)S(1)}, bf16[128,1792]{1,0:T(8,128)(2,1)S(1)}, u32[]{:S(2)}, u32[]{:S(2)}) collective-permute-start(bf16[128,1792]{1,0:T(8,128)(2,1)S(1)} %get-tuple-element.73.img_ref), channel_id=1, source_target_pairs={{0,64},{1,193},{32,96},{33,225},{64,128},{65,1},{96,160},{97,33},{... | collective-permute-start | bytes 1376264 | tf_op jit(solution)/shard_map/ppermute | solution.py:394
  14.1 2.4 %collective-permute-done.6.d_ref = bf16[64,1792]{1,0:T(8,128)(2,1)S(1)} collective-permute-done((bf16[64,1792]{1,0:T(8,128)(2,1)S(1)}, bf16[64,1792]{1,0:T(8,128)(2,1)S(1)}, u32[]{:S(2)}, u32[]{:S(2)}) %collective-permute-start.6) | collective-permute-done | bytes 229408 | tf_op jit(solution)/shard_map/ppermute | solution.py:390
  18.2 8.1 %collective-permute-done.8.two_ref = bf16[128,1792]{1,0:T(8,128)(2,1)S(1)} collective-permute-done((bf16[128,1792]{1,0:T(8,128)(2,1)S(1)}, bf16[128,1792]{1,0:T(8,128)(2,1)S(1)}, u32[]{:S(2)}, u32[]{:S(2)}) %collective-permute-start.8) | collective-permute-done | bytes 458784 | tf_op jit(solution)/shard_map/ppermute | solution.py:394
  27.1 2.4 %collective-permute-start.9 = (bf16[192,1792]{1,0:T(8,128)(2,1)S(1)}, bf16[192,1792]{1,0:T(8,128)(2,1)S(1)}, u32[]{:S(2)}, u32[]{:S(2)}) collective-permute-start(bf16[192,1792]{1,0:T(8,128)(2,1)S(1)} %get-tuple-element.75), channel_id=1, source_target_pairs={{0,64},{1,193},{32,96},{33,225},{64,128},{65,1},{96,160},{97,33},{... | collective-permute-start | bytes 2064392 | tf_op jit(solution)/shard_map/ppermute | solution.py:394
  33.0 2.0 %collective-permute-start.13 = (bf16[256,1792]{1,0:T(8,128)(2,1)S(1)}, bf16[256,1792]{1,0:T(8,128)(2,1)S(1)}, u32[]{:S(2)}, u32[]{:S(2)}) collective-permute-start(bf16[256,1792]{1,0:T(8,128)(2,1)S(1)} %collective-permute-done.12.refs_0_), channel_id=1, source_target_pairs={{0,4},{1,3},{2,6},{3,17},{4,8},{5,7},{6,10},{7,21},{8,12},{9,11},{... | collective-permute-start | bytes 2752520 | tf_op jit(solution)/shard_map/ppermute | solution.py:390
  35.0 7.9 %collective-permute-done.9.ahead_ref = bf16[192,1792]{1,0:T(8,128)(2,1)S(1)} collective-permute-done((bf16[192,1792]{1,0:T(8,128)(2,1)S(1)}, bf16[192,1792]{1,0:T(8,128)(2,1)S(1)}, u32[]{:S(2)}, u32[]{:S(2)}) %collective-permute-start.9) | collective-permute-done | bytes 688160 | tf_op jit(solution)/shard_map/ppermute | solution.py:394
  42.9 4.0 %collective-permute-start.10 = (bf16[64,1792]{1,0:T(8,128)(2,1)S(1)}, bf16[64,1792]{1,0:T(8,128)(2,1)S(1)}, u32[]{:S(2)}, u32[]{:S(2)}) collective-permute-start(bf16[64,1792]{1,0:T(8,128)(2,1)S(1)} %slice.12), channel_id=1, source_target_pairs={{0,1},{1,0},{2,3},{3,2},{4,5},{5,4},{6,7},{7,6},{8,9},{9,8},{10,11... | collective-permute-start | bytes 688136 | tf_op jit(solution)/shard_map/ppermute | solution.py:364
  49.2 2.1 %block0.1 = (bf16[512,2048]{1,0:T(8,128)(2,1)S(1)}, bf16[512,2048]{1,0:T(8,128)(2,1)S(1)}, bf16[512,2048]{1,0:T(8,128)(2,1)S(1)}, bf16[2048,768]{1,0:T(8,128)(2,...) custom-call(bf16[512,1024]{1,0:T(8,128)(2,1)S(1)} %get-tuple-element.88.timg_ref, ...), custom_call_target="tpu_custom_call" | custom-call | flops 1 | bytes 1 | tf_op jit(solution)/shard_map/block0/pallas_call | solution.py:455
  51.3 2.6 %block1.1 = (bf16[512,2048]{1,0:T(8,128)(2,1)S(1)}, bf16[512,2048]{1,0:T(8,128)(2,1)S(1)}, bf16[512,2048]{1,0:T(8,128)(2,1)S(1)}, bf16[2048,768]{1,0:T(8,128)(2,...) custom-call(bf16[512,1024]{1,0:T(8,128)(2,1)S(1)} %get-tuple-element, ...), custom_call_target="tpu_custom_call", output_to_operand_aliasing={{0}: (5, {}), {1}: (6, {}), {2}: (7, {}), {3}: (8, {}), {4}... | custom-call | flops 1 | bytes 1 | tf_op jit(solution)/shard_map/block1/pallas_call | solution.py:455
  54.4 2.6 %block2.1 = (bf16[512,2048]{1,0:T(8,128)(2,1)S(1)}, bf16[512,2048]{1,0:T(8,128)(2,1)S(1)}, bf16[512,2048]{1,0:T(8,128)(2,1)S(1)}, bf16[2048,768]{1,0:T(8,128)(2,...) custom-call(bf16[512,1024]{1,0:T(8,128)(2,1)S(1)} %get-tuple-element, ...), custom_call_target="tpu_custom_call", output_to_operand_aliasing={{0}: (5, {}), {1}: (6, {}), {2}: (7, {}), {3}: (8, {}), {4}... | custom-call | flops 1 | bytes 1 | tf_op jit(solution)/shard_map/block2/pallas_call | solution.py:455
  57.0 3.5 %block3.1 = (bf16[512,2048]{1,0:T(8,128)(2,1)S(1)}, bf16[512,2048]{1,0:T(8,128)(2,1)S(1)}, bf16[512,2048]{1,0:T(8,128)(2,1)S(1)}, bf16[2048,768]{1,0:T(8,128)(2,...) custom-call(bf16[512,1024]{1,0:T(8,128)(2,1)S(1)} %get-tuple-element, ...), custom_call_target="tpu_custom_call", output_to_operand_aliasing={{0}: (5, {}), {1}: (6, {}), {2}: (7, {}), {3}: (8, {}), {4}... | custom-call | flops 1 | bytes 1 | tf_op jit(solution)/shard_map/block3/pallas_call | solution.py:455
  60.5 3.0 %collective-permute-start.19 = (f32[8,512]{1,0:T(8,128)S(1)}, f32[8,512]{1,0:T(8,128)S(1)}, u32[]{:S(2)}, u32[]{:S(2)}) collective-permute-start(f32[8,512]{1,0:T(8,128)S(1)} %get-tuple-element.109.own_ref.flat_ref), channel_id=1, source_target_pairs={{0,224},{32,0},{64,32},{96,64},{128,96},{160,128},{192,160},{224,1... | collective-permute-start | bytes 49160 | tf_op jit(solution)/shard_map/ppermute | solution.py:494
  63.5 4.1 %student.1 = (bf16[512,768]{1,0:T(8,128)(2,1)S(1)}, bf16[512,768]{1,0:T(8,128)(2,1)S(1)}, bf16[768,512]{1,0:T(8,128)(2,1)S(1)}, f32[8,128]{1,0:T(8,128)S(1)}) custom-call(bf16[512,2048]{1,0:T(8,128)(2,1)S(1)} %get-tuple-element.110.se_ref, bf16[512,2048]{1,0:T(8,128)(2,1)S(1)} %get-tuple-element.111.sig_ref, ...), custom_call_target="tpu_custom_call" | custom-call | flops 1 | bytes 1 | tf_op jit(solution)/shard_map/student/pallas_call | solution.py:473
  68.5 4.1 %collective-permute-start.21 = (f32[8,512]{1,0:T(8,128)S(1)}, f32[8,512]{1,0:T(8,128)S(1)}, u32[]{:S(2)}, u32[]{:S(2)}) collective-permute-start(f32[8,512]{1,0:T(8,128)S(1)} %get-tuple-element.117.window_ref), channel_id=1, source_target_pairs={{0,160},{32,192},{64,224},{96,0},{128,32},{160,64},{192,96},{224,1... | collective-permute-start | bytes 49160 | tf_op jit(solution)/shard_map/ppermute | solution.py:503
  73.0 2.4 %teacher.1.b_ref = bf16[512,768]{1,0:T(8,128)(2,1)S(1)} custom-call(bf16[512,2048]{1,0:T(8,128)(2,1)S(1)} %get-tuple-element.120.te_ref, bf16[2048,768]{1,0:T(8,128)(2,1)S(1)} %get-tuple-element.112.stu_ref, f32[512,768]{1,0:T(8,128)S(1)} %get-tuple-element.113.simg_ref, f32[512,128]{1,0:T(8,128)S(1)} %get-tuple-element.114.inv_ref, ...), custom_call_target="tpu_custom_call" | custom-call | flops 1 | bytes 1 | tf_op jit(solution)/shard_map/teacher/pallas_call | solution.py:482
  75.5 3.9 %collective-permute-done.22.behind_ref = f32[8,512]{1,0:T(8,128)S(1)} collective-permute-done((f32[8,512]{1,0:T(8,128)S(1)}, f32[8,512]{1,0:T(8,128)S(1)}, u32[]{:S(2)}, u32[]{:S(2)}) %collective-permute-start.22) | collective-permute-done | bytes 16416 | tf_op jit(solution)/shard_map/ppermute | solution.py:504
  79.4 2.4 %away.1 = (f32[392,768]{1,0:T(8,128)S(1)}, bf16[512,768]{1,0:T(8,128)(2,1)S(1)}, bf16[512,768]{1,0:T(8,128)(2,1)S(1)}, f32[8,512]{1,0:T(8,128)S(1)}) custom-call(s32[4]{0:T(128)S(1)} %pad_add_fusion.place_ref, f32[8,512]{1,0:T(8,128)S(1)} %get-tuple-element.117.window_ref, f32[8,512]{1,0:T(8,128)S(1)} %collective-permute-done.21.ahead_ref, ...), custom_call_target="tpu_custom_call" | custom-call | flops 1 | bytes 1 | tf_op jit(solution)/shard_map/away/pallas_call | solution.py:506
  90.3 3.1 %collective-permute-done.24.p_ref = bf16[112,768]{1,0:T(8,128)(2,1)S(1)} collective-permute-done((bf16[112,768]{1,0:T(8,128)(2,1)S(1)}, bf16[112,768]{1,0:T(8,128)(2,1)S(1)}, u32[]{:S(2)}, u32[]{:S(2)}) %collective-permute-start.24) | collective-permute-done | bytes 172064 | tf_op jit(solution)/shard_map/ppermute | solution.py:537
  93.4 5.0 %collective-permute-done.26.r_ref = bf16[112,768]{1,0:T(8,128)(2,1)S(1)} collective-permute-done((bf16[112,768]{1,0:T(8,128)(2,1)S(1)}, bf16[112,768]{1,0:T(8,128)(2,1)S(1)}, u32[]{:S(2)}, u32[]{:S(2)}) %collective-permute-start.26) | collective-permute-done | bytes 172064 | tf_op jit(solution)/shard_map/ppermute | solution.py:537
  102.7 5.8 %collective-permute-done.29.r_ref = bf16[64,768]{1,0:T(8,128)(2,1)S(1)} collective-permute-done((bf16[64,768]{1,0:T(8,128)(2,1)S(1)}, bf16[64,768]{1,0:T(8,128)(2,1)S(1)}, u32[]{:S(2)}, u32[]{:S(2)}) %collective-permute-start.29) | collective-permute-done | bytes 98336 | tf_op jit(solution)/shard_map/ppermute | solution.py:555
  110.6 3.1 %collective-permute-done.30 = f32[48,768]{1,0:T(8,128)S(1)} collective-permute-done((f32[48,768]{1,0:T(8,128)S(1)}, f32[48,768]{1,0:T(8,128)S(1)}, u32[]{:S(2)}, u32[]{:S(2)}) %collective-permute-start.30) | collective-permute-done | bytes 147488 | tf_op jit(solution)/shard_map/ppermute | solution.py:558
  113.7 2.0 %collective-permute-done.31 = f32[48,768]{1,0:T(8,128)S(1)} collective-permute-done((f32[48,768]{1,0:T(8,128)S(1)}, f32[48,768]{1,0:T(8,128)S(1)}, u32[]{:S(2)}, u32[]{:S(2)}) %collective-permute-start.31) | collective-permute-done | bytes 147488 | tf_op jit(solution)/shard_map/ppermute | solution.py:557
  116.2 3.5 %collective-permute-start.33 = (bf16[48,768]{1,0:T(8,128)(2,1)S(1)}, bf16[48,768]{1,0:T(8,128)(2,1)S(1)}, u32[]{:S(2)}, u32[]{:S(2)}) collective-permute-start(bf16[48,768]{1,0:T(8,128)(2,1)S(1)} %get-tuple-element.142), channel_id=1, source_target_pairs={{0,96},{32,128},{64,160},{96,192},{128,224},{160,0},{192,32},{224,... | collective-permute-start | bytes 221192 | tf_op jit(solution)/shard_map/ppermute | solution.py:562
  (71 shorter events, 37.5 us)
Async XLA Ops:
  3.6 12.9 %collective-permute-start.7 = (bf16[128,1792]{1,0:T(8,128)(2,1)S(1)}, bf16[128,1792]{1,0:T(8,128)(2,1)S(1)}, u32[]{:S(2)}, u32[]{:S(2)}) collective-permute-start(bf16[128,1792]{1,0:T(8,128)(2,1)S(1)} %get-tuple-element.73.img_ref), channel_id=1, source_target_pairs={{0,32},{1,225},{32,64},{33,1},{64,96},{65,33},{96,128},{97,65},{12... | collective-permute-start | bytes 1376264 | tf_op jit(solution)/shard_map/ppermute | solution.py:394
  5.6 8.5 %collective-permute-start.4 = (bf16[64,1792]{1,0:T(8,128)(2,1)S(1)}, bf16[64,1792]{1,0:T(8,128)(2,1)S(1)}, u32[]{:S(2)}, u32[]{:S(2)}) collective-permute-start(bf16[64,1792]{1,0:T(8,128)(2,1)S(1)} %get-tuple-element.72.a_ref), channel_id=1, source_target_pairs={{0,2},{1,5},{2,16},{3,7},{4,6},{5,9},{6,20},{7,11},{8,10},{9,13},{... | collective-permute-start | bytes 688136 | tf_op jit(solution)/shard_map/ppermute | solution.py:390
  7.2 6.9 %collective-permute-start.5 = (bf16[64,1792]{1,0:T(8,128)(2,1)S(1)}, bf16[64,1792]{1,0:T(8,128)(2,1)S(1)}, u32[]{:S(2)}, u32[]{:S(2)}) collective-permute-start(bf16[64,1792]{1,0:T(8,128)(2,1)S(1)} %get-tuple-element.72.a_ref), channel_id=1, source_target_pairs={{0,18},{1,13},{2,0},{3,15},{4,22},{5,1},{6,4},{7,3},{8,26},{9,5},{... | collective-permute-start | bytes 688136 | tf_op jit(solution)/shard_map/ppermute | solution.py:390
  8.9 7.7 %collective-permute-start.6 = (bf16[64,1792]{1,0:T(8,128)(2,1)S(1)}, bf16[64,1792]{1,0:T(8,128)(2,1)S(1)}, u32[]{:S(2)}, u32[]{:S(2)}) collective-permute-start(bf16[64,1792]{1,0:T(8,128)(2,1)S(1)} %get-tuple-element.72.a_ref), channel_id=1, source_target_pairs={{0,16},{1,9},{2,18},{3,11},{4,20},{5,13},{6,22},{7,15},{8,24},{9,1... | collective-permute-start | bytes 688136 | tf_op jit(solution)/shard_map/ppermute | solution.py:390
  10.8 15.4 %collective-permute-start.8 = (bf16[128,1792]{1,0:T(8,128)(2,1)S(1)}, bf16[128,1792]{1,0:T(8,128)(2,1)S(1)}, u32[]{:S(2)}, u32[]{:S(2)}) collective-permute-start(bf16[128,1792]{1,0:T(8,128)(2,1)S(1)} %get-tuple-element.73.img_ref), channel_id=1, source_target_pairs={{0,64},{1,193},{32,96},{33,225},{64,128},{65,1},{96,160},{97,33},{... | collective-permute-start | bytes 1376264 | tf_op jit(solution)/shard_map/ppermute | solution.py:394
  16.6 15.3 %collective-permute-start.12 = (bf16[256,1792]{1,0:T(8,128)(2,1)S(1)}, bf16[256,1792]{1,0:T(8,128)(2,1)S(1)}, u32[]{:S(2)}, u32[]{:S(2)}) collective-permute-start(bf16[256,1792]{1,0:T(8,128)(2,1)S(1)} %column.1.refs_0_), channel_id=1, source_target_pairs={{0,4},{1,3},{2,6},{3,17},{4,8},{5,7},{6,10},{7,21},{8,12},{9,11},{... | collective-permute-start | bytes 2752520 | tf_op jit(solution)/shard_map/ppermute | solution.py:390
  26.5 20.5 %collective-permute-start.16 = (bf16[256,1792]{1,0:T(8,128)(2,1)S(1)}, bf16[256,1792]{1,0:T(8,128)(2,1)S(1)}, u32[]{:S(2)}, u32[]{:S(2)}) collective-permute-start(bf16[256,1792]{1,0:T(8,128)(2,1)S(1)} %column.1.refs_0_), channel_id=1, source_target_pairs={{0,12},{1,19},{2,14},{3,1},{4,0},{5,23},{6,2},{7,5},{8,4},{9,27},{... | collective-permute-start | bytes 2752520 | tf_op jit(solution)/shard_map/ppermute | solution.py:390
  27.1 15.8 %collective-permute-start.9 = (bf16[192,1792]{1,0:T(8,128)(2,1)S(1)}, bf16[192,1792]{1,0:T(8,128)(2,1)S(1)}, u32[]{:S(2)}, u32[]{:S(2)}) collective-permute-start(bf16[192,1792]{1,0:T(8,128)(2,1)S(1)} %get-tuple-element.75), channel_id=1, source_target_pairs={{0,64},{1,193},{32,96},{33,225},{64,128},{65,1},{96,160},{97,33},{... | collective-permute-start | bytes 2064392 | tf_op jit(solution)/shard_map/ppermute | solution.py:394
  29.5 19.7 %collective-permute-start.14 = (bf16[256,1792]{1,0:T(8,128)(2,1)S(1)}, bf16[256,1792]{1,0:T(8,128)(2,1)S(1)}, u32[]{:S(2)}, u32[]{:S(2)}) collective-permute-start(bf16[256,1792]{1,0:T(8,128)(2,1)S(1)} %column.1.refs_0_), channel_id=1, source_target_pairs={{0,1},{1,0},{2,3},{3,2},{4,5},{5,4},{6,7},{7,6},{8,9},{9,8},{10,11... | collective-permute-start | bytes 2752520 | tf_op jit(solution)/shard_map/ppermute | solution.py:364
  31.9 19.4 %collective-permute-start.15 = (bf16[256,1792]{1,0:T(8,128)(2,1)S(1)}, bf16[256,1792]{1,0:T(8,128)(2,1)S(1)}, u32[]{:S(2)}, u32[]{:S(2)}) collective-permute-start(bf16[256,1792]{1,0:T(8,128)(2,1)S(1)} %collective-permute-done.12.refs_0_), channel_id=1, source_target_pairs={{0,1},{1,0},{2,3},{3,2},{4,5},{5,4},{6,7},{7,6},{8,9},{9,8},{10,11... | collective-permute-start | bytes 2752520 | tf_op jit(solution)/shard_map/ppermute | solution.py:364
  33.0 20.9 %collective-permute-start.13 = (bf16[256,1792]{1,0:T(8,128)(2,1)S(1)}, bf16[256,1792]{1,0:T(8,128)(2,1)S(1)}, u32[]{:S(2)}, u32[]{:S(2)}) collective-permute-start(bf16[256,1792]{1,0:T(8,128)(2,1)S(1)} %collective-permute-done.12.refs_0_), channel_id=1, source_target_pairs={{0,4},{1,3},{2,6},{3,17},{4,8},{5,7},{6,10},{7,21},{8,12},{9,11},{... | collective-permute-start | bytes 2752520 | tf_op jit(solution)/shard_map/ppermute | solution.py:390
  46.9 7.4 %collective-permute-start.17 = (bf16[256,1792]{1,0:T(8,128)(2,1)S(1)}, bf16[256,1792]{1,0:T(8,128)(2,1)S(1)}, u32[]{:S(2)}, u32[]{:S(2)}) collective-permute-start(bf16[256,1792]{1,0:T(8,128)(2,1)S(1)} %collective-permute-done.16.refs_0_), channel_id=1, source_target_pairs={{0,1},{1,0},{2,3},{3,2},{4,5},{5,4},{6,7},{7,6},{8,9},{9,8},{10,11... | collective-permute-start | bytes 2752520 | tf_op jit(solution)/shard_map/ppermute | solution.py:364
  60.5 7.1 %collective-permute-start.19 = (f32[8,512]{1,0:T(8,128)S(1)}, f32[8,512]{1,0:T(8,128)S(1)}, u32[]{:S(2)}, u32[]{:S(2)}) collective-permute-start(f32[8,512]{1,0:T(8,128)S(1)} %get-tuple-element.109.own_ref.flat_ref), channel_id=1, source_target_pairs={{0,224},{32,0},{64,32},{96,64},{128,96},{160,128},{192,160},{224,1... | collective-permute-start | bytes 49160 | tf_op jit(solution)/shard_map/ppermute | solution.py:494
  68.5 6.9 %collective-permute-start.21 = (f32[8,512]{1,0:T(8,128)S(1)}, f32[8,512]{1,0:T(8,128)S(1)}, u32[]{:S(2)}, u32[]{:S(2)}) collective-permute-start(f32[8,512]{1,0:T(8,128)S(1)} %get-tuple-element.117.window_ref), channel_id=1, source_target_pairs={{0,160},{32,192},{64,224},{96,0},{128,32},{160,64},{192,96},{224,1... | collective-permute-start | bytes 49160 | tf_op jit(solution)/shard_map/ppermute | solution.py:503
  72.6 6.7 %collective-permute-start.22 = (f32[8,512]{1,0:T(8,128)S(1)}, f32[8,512]{1,0:T(8,128)S(1)}, u32[]{:S(2)}, u32[]{:S(2)}) collective-permute-start(f32[8,512]{1,0:T(8,128)S(1)} %get-tuple-element.118), channel_id=1, source_target_pairs={{0,96},{32,128},{64,160},{96,192},{128,224},{160,0},{192,32},{224,... | collective-permute-start | bytes 49160 | tf_op jit(solution)/shard_map/ppermute | solution.py:504
  85.4 8.0 %collective-permute-start.24 = (bf16[112,768]{1,0:T(8,128)(2,1)S(1)}, bf16[112,768]{1,0:T(8,128)(2,1)S(1)}, u32[]{:S(2)}, u32[]{:S(2)}) collective-permute-start(bf16[112,768]{1,0:T(8,128)(2,1)S(1)} %get-tuple-element.133), channel_id=1, source_target_pairs={{0,4},{4,8},{8,12},{12,0},{1,5},{5,9},{9,13},{13,1},{2,6},{6,10},{... | collective-permute-start | bytes 516104 | tf_op jit(solution)/shard_map/ppermute | solution.py:537
  86.9 6.4 %collective-permute-start.25 = (bf16[112,768]{1,0:T(8,128)(2,1)S(1)}, bf16[112,768]{1,0:T(8,128)(2,1)S(1)}, u32[]{:S(2)}, u32[]{:S(2)}) collective-permute-start(bf16[112,768]{1,0:T(8,128)(2,1)S(1)} %get-tuple-element.134), channel_id=1, source_target_pairs={{0,12},{4,0},{8,4},{12,8},{1,13},{5,1},{9,5},{13,9},{2,14},{6,2},{... | collective-permute-start | bytes 516104 | tf_op jit(solution)/shard_map/ppermute | solution.py:537
  88.3 10.1 %collective-permute-start.26 = (bf16[112,768]{1,0:T(8,128)(2,1)S(1)}, bf16[112,768]{1,0:T(8,128)(2,1)S(1)}, u32[]{:S(2)}, u32[]{:S(2)}) collective-permute-start(bf16[112,768]{1,0:T(8,128)(2,1)S(1)} %get-tuple-element.135), channel_id=1, source_target_pairs={{0,8},{4,12},{8,0},{12,4},{1,9},{5,13},{9,1},{13,5},{2,10},{6,14},... | collective-permute-start | bytes 516104 | tf_op jit(solution)/shard_map/ppermute | solution.py:537
  99.0 9.4 %collective-permute-start.27 = (f32[56,768]{1,0:T(8,128)S(1)}, f32[56,768]{1,0:T(8,128)S(1)}, u32[]{:S(2)}, u32[]{:S(2)}) collective-permute-start(f32[56,768]{1,0:T(8,128)S(1)} %get-tuple-element.137), channel_id=1, source_target_pairs={{0,2},{2,16},{16,18},{18,0},{1,3},{3,17},{17,19},{19,1},{4,6},{6,2... | collective-permute-start | bytes 516104 | tf_op jit(solution)/shard_map/ppermute | solution.py:555
  100.5 7.9 %collective-permute-start.28 = (f32[56,768]{1,0:T(8,128)S(1)}, f32[56,768]{1,0:T(8,128)S(1)}, u32[]{:S(2)}, u32[]{:S(2)}) collective-permute-start(f32[56,768]{1,0:T(8,128)S(1)} %get-tuple-element.137), channel_id=1, source_target_pairs={{0,18},{2,0},{16,2},{18,16},{1,19},{3,1},{17,3},{19,17},{4,22},{6,... | collective-permute-start | bytes 516104 | tf_op jit(solution)/shard_map/ppermute | solution.py:555
  102.3 6.1 %collective-permute-start.29 = (bf16[64,768]{1,0:T(8,128)(2,1)S(1)}, bf16[64,768]{1,0:T(8,128)(2,1)S(1)}, u32[]{:S(2)}, u32[]{:S(2)}) collective-permute-start(bf16[64,768]{1,0:T(8,128)(2,1)S(1)} %get-tuple-element.138), channel_id=1, source_target_pairs={{0,16},{2,18},{16,0},{18,2},{1,17},{3,19},{17,1},{19,3},{4,20},{6,... | collective-permute-start | bytes 294920 | tf_op jit(solution)/shard_map/ppermute | solution.py:555
  109.4 6.4 %collective-permute-start.31 = (f32[48,768]{1,0:T(8,128)S(1)}, f32[48,768]{1,0:T(8,128)S(1)}, u32[]{:S(2)}, u32[]{:S(2)}) collective-permute-start(f32[48,768]{1,0:T(8,128)S(1)} %get-tuple-element.140), channel_id=1, source_target_pairs={{0,32},{32,64},{64,96},{96,128},{128,160},{160,192},{192,224},{224... | collective-permute-start | bytes 442376 | tf_op jit(solution)/shard_map/ppermute | solution.py:557
  115.8 7.1 %collective-permute-start.32 = (bf16[48,768]{1,0:T(8,128)(2,1)S(1)}, bf16[48,768]{1,0:T(8,128)(2,1)S(1)}, u32[]{:S(2)}, u32[]{:S(2)}) collective-permute-start(bf16[48,768]{1,0:T(8,128)(2,1)S(1)} %get-tuple-element.141), channel_id=1, source_target_pairs={{0,160},{32,192},{64,224},{96,0},{128,32},{160,64},{192,96},{224,1... | collective-permute-start | bytes 221192 | tf_op jit(solution)/shard_map/ppermute | solution.py:561
  116.2 7.4 %collective-permute-start.33 = (bf16[48,768]{1,0:T(8,128)(2,1)S(1)}, bf16[48,768]{1,0:T(8,128)(2,1)S(1)}, u32[]{:S(2)}, u32[]{:S(2)}) collective-permute-start(bf16[48,768]{1,0:T(8,128)(2,1)S(1)} %get-tuple-element.142), channel_id=1, source_target_pairs={{0,96},{32,128},{64,160},{96,192},{128,224},{160,0},{192,32},{224,... | collective-permute-start | bytes 221192 | tf_op jit(solution)/shard_map/ppermute | solution.py:562
  (11 other events, 62.9 us)

commit v3 on v2

--- a/solution.py
+++ b/solution.py
@@ -188,11 +188,9 @@
 
         lax.fori_loop(0, images // GROUP, body, 0)
         if last:
-            ones = jnp.ones((8, LANES), F32)
             out = [stat_ref[:, :LANES].T[:1, :]]
             for k in range(1, 5):
-                v = lax.dot_general(ones, stat_ref[:, k * LANES:(k + 1) * LANES], NT, precision=lax.Precision.HIGHEST, preferred_element_type=F32)
-                out.append(v[:1, :])
+                out.append(jnp.sum(stat_ref[:, k * LANES:(k + 1) * LANES].T, axis=0, keepdims=True))
             flat_ref[...] = jnp.concatenate(out + [jnp.zeros((3, images), F32)], axis=0)
 
     return kernel

time: 127 us -> 127 us (level)
  no operation moved by 1% of the time
where the time goes in v3:
time: 127 us; the launch traced here: 125 us
  starting transfers between devices  47.1 us (37%)
  waiting for transfers between devices  46.9 us (37%)
  Pallas kernels  25.3 us (20%)
  between operations  2.66 us (2%)
  other arithmetic  1.9 us (1%)
    ppermute x3, waiting for transfers between devices, climb(): return lax.ppermute(v, ('z', 'c'), pairs)  16 us
    pallas_call x4, Pallas kernels, per_device(): pl.pallas_call(make_block(n, final, gain, [v.shape[0] for v in block]), i...  10.3 us
    ppermute x6, starting transfers between devices, plane(): return lax.ppermute(v, ('yh', 'x', 'yl', 'c'), pairs)  9.41 us
    ppermute x3, waiting for transfers between devices, per_device(): got = [lax.ppermute(v, 'x', ring(xn, k)) for k, v in zip((1, 3, 2), sends)]  8.08 us
    ppermute x11, starting transfers between devices, per_device(): swap = lambda v: lax.ppermute(v, 'c', flip(cn, 1))  7.89 us
    ppermute x3, starting transfers between devices, climb(): return lax.ppermute(v, ('z', 'c'), pairs)  7.66 us
    ppermute x1, waiting for transfers between devices, per_device(): lax.ppermute(across, Y, ring(yn, 2))  5.76 us
    ppermute x3, starting transfers between devices, per_device(): got = [lax.ppermute(v, 'x', ring(xn, k)) for k, v in zip((1, 3, 2), sends)]  4.91 us
  transfers between devices with their start and end apart: 34, of which 14 were waited for; matrix products, arithmetic and copies ran while one was open for 2% of the time, Pallas kernels for 14%

profile of v3, /device:TPU:2, one launch (start us, length us, event | category | flops | bytes accessed | tf_op | source)
XLA Modules:
  0.0 124.9 jit_solution(17754803214617349736)
XLA Ops:
  3.6 2.0 %collective-permute-start.7 = (bf16[128,1792]{1,0:T(8,128)(2,1)S(1)}, bf16[128,1792]{1,0:T(8,128)(2,1)S(1)}, u32[]{:S(2)}, u32[]{:S(2)}) collective-permute-start(bf16[128,1792]{1,0:T(8,128)(2,1)S(1)} %get-tuple-element.73.img_ref), channel_id=1, source_target_pairs={{0,32},{1,225},{32,64},{33,1},{64,96},{65,33},{96,128},{97,65},{12... | collective-permute-start | bytes 1376264 | tf_op jit(solution)/shard_map/ppermute | solution.py:392
  10.8 3.3 %collective-permute-start.8 = (bf16[128,1792]{1,0:T(8,128)(2,1)S(1)}, bf16[128,1792]{1,0:T(8,128)(2,1)S(1)}, u32[]{:S(2)}, u32[]{:S(2)}) collective-permute-start(bf16[128,1792]{1,0:T(8,128)(2,1)S(1)} %get-tuple-element.73.img_ref), channel_id=1, source_target_pairs={{0,64},{1,193},{32,96},{33,225},{64,128},{65,1},{96,160},{97,33},{... | collective-permute-start | bytes 1376264 | tf_op jit(solution)/shard_map/ppermute | solution.py:392
  14.1 2.4 %collective-permute-done.6.d_ref = bf16[64,1792]{1,0:T(8,128)(2,1)S(1)} collective-permute-done((bf16[64,1792]{1,0:T(8,128)(2,1)S(1)}, bf16[64,1792]{1,0:T(8,128)(2,1)S(1)}, u32[]{:S(2)}, u32[]{:S(2)}) %collective-permute-start.6) | collective-permute-done | bytes 229408 | tf_op jit(solution)/shard_map/ppermute | solution.py:388
  18.2 8.1 %collective-permute-done.8.two_ref = bf16[128,1792]{1,0:T(8,128)(2,1)S(1)} collective-permute-done((bf16[128,1792]{1,0:T(8,128)(2,1)S(1)}, bf16[128,1792]{1,0:T(8,128)(2,1)S(1)}, u32[]{:S(2)}, u32[]{:S(2)}) %collective-permute-start.8) | collective-permute-done | bytes 458784 | tf_op jit(solution)/shard_map/ppermute | solution.py:392
  27.1 2.4 %collective-permute-start.9 = (bf16[192,1792]{1,0:T(8,128)(2,1)S(1)}, bf16[192,1792]{1,0:T(8,128)(2,1)S(1)}, u32[]{:S(2)}, u32[]{:S(2)}) collective-permute-start(bf16[192,1792]{1,0:T(8,128)(2,1)S(1)} %get-tuple-element.75), channel_id=1, source_target_pairs={{0,64},{1,193},{32,96},{33,225},{64,128},{65,1},{96,160},{97,33},{... | collective-permute-start | bytes 2064392 | tf_op jit(solution)/shard_map/ppermute | solution.py:392
  33.0 2.0 %collective-permute-start.13 = (bf16[256,1792]{1,0:T(8,128)(2,1)S(1)}, bf16[256,1792]{1,0:T(8,128)(2,1)S(1)}, u32[]{:S(2)}, u32[]{:S(2)}) collective-permute-start(bf16[256,1792]{1,0:T(8,128)(2,1)S(1)} %collective-permute-done.12.refs_0_), channel_id=1, source_target_pairs={{0,4},{1,3},{2,6},{3,17},{4,8},{5,7},{6,10},{7,21},{8,12},{9,11},{... | collective-permute-start | bytes 2752520 | tf_op jit(solution)/shard_map/ppermute | solution.py:388
  35.0 7.9 %collective-permute-done.9.ahead_ref = bf16[192,1792]{1,0:T(8,128)(2,1)S(1)} collective-permute-done((bf16[192,1792]{1,0:T(8,128)(2,1)S(1)}, bf16[192,1792]{1,0:T(8,128)(2,1)S(1)}, u32[]{:S(2)}, u32[]{:S(2)}) %collective-permute-start.9) | collective-permute-done | bytes 688160 | tf_op jit(solution)/shard_map/ppermute | solution.py:392
  42.9 4.0 %collective-permute-start.10 = (bf16[64,1792]{1,0:T(8,128)(2,1)S(1)}, bf16[64,1792]{1,0:T(8,128)(2,1)S(1)}, u32[]{:S(2)}, u32[]{:S(2)}) collective-permute-start(bf16[64,1792]{1,0:T(8,128)(2,1)S(1)} %slice.12), channel_id=1, source_target_pairs={{0,1},{1,0},{2,3},{3,2},{4,5},{5,4},{6,7},{7,6},{8,9},{9,8},{10,11... | collective-permute-start | bytes 688136 | tf_op jit(solution)/shard_map/ppermute | solution.py:362
  49.2 2.1 %block0.1 = (bf16[512,2048]{1,0:T(8,128)(2,1)S(1)}, bf16[512,2048]{1,0:T(8,128)(2,1)S(1)}, bf16[512,2048]{1,0:T(8,128)(2,1)S(1)}, bf16[2048,768]{1,0:T(8,128)(2,...) custom-call(bf16[512,1024]{1,0:T(8,128)(2,1)S(1)} %get-tuple-element.88.timg_ref, ...), custom_call_target="tpu_custom_call" | custom-call | flops 1 | bytes 1 | tf_op jit(solution)/shard_map/block0/pallas_call | solution.py:453
  51.3 2.6 %block1.1 = (bf16[512,2048]{1,0:T(8,128)(2,1)S(1)}, bf16[512,2048]{1,0:T(8,128)(2,1)S(1)}, bf16[512,2048]{1,0:T(8,128)(2,1)S(1)}, bf16[2048,768]{1,0:T(8,128)(2,...) custom-call(bf16[512,1024]{1,0:T(8,128)(2,1)S(1)} %get-tuple-element, ...), custom_call_target="tpu_custom_call", output_to_operand_aliasing={{0}: (5, {}), {1}: (6, {}), {2}: (7, {}), {3}: (8, {}), {4}... | custom-call | flops 1 | bytes 1 | tf_op jit(solution)/shard_map/block1/pallas_call | solution.py:453
  54.4 2.6 %block2.1 = (bf16[512,2048]{1,0:T(8,128)(2,1)S(1)}, bf16[512,2048]{1,0:T(8,128)(2,1)S(1)}, bf16[512,2048]{1,0:T(8,128)(2,1)S(1)}, bf16[2048,768]{1,0:T(8,128)(2,...) custom-call(bf16[512,1024]{1,0:T(8,128)(2,1)S(1)} %get-tuple-element, ...), custom_call_target="tpu_custom_call", output_to_operand_aliasing={{0}: (5, {}), {1}: (6, {}), {2}: (7, {}), {3}: (8, {}), {4}... | custom-call | flops 1 | bytes 1 | tf_op jit(solution)/shard_map/block2/pallas_call | solution.py:453
  57.0 3.0 %block3.1 = (bf16[512,2048]{1,0:T(8,128)(2,1)S(1)}, bf16[512,2048]{1,0:T(8,128)(2,1)S(1)}, bf16[512,2048]{1,0:T(8,128)(2,1)S(1)}, bf16[2048,768]{1,0:T(8,128)(2,...) custom-call(bf16[512,1024]{1,0:T(8,128)(2,1)S(1)} %get-tuple-element, ...), custom_call_target="tpu_custom_call", output_to_operand_aliasing={{0}: (5, {}), {1}: (6, {}), {2}: (7, {}), {3}: (8, {}), {4}... | custom-call | flops 1 | bytes 1 | tf_op jit(solution)/shard_map/block3/pallas_call | solution.py:453
  60.0 3.1 %collective-permute-start.19 = (f32[8,512]{1,0:T(8,128)S(1)}, f32[8,512]{1,0:T(8,128)S(1)}, u32[]{:S(2)}, u32[]{:S(2)}) collective-permute-start(f32[8,512]{1,0:T(8,128)S(1)} %get-tuple-element.109.own_ref.flat_ref), channel_id=1, source_target_pairs={{0,224},{32,0},{64,32},{96,64},{128,96},{160,128},{192,160},{224,1... | collective-permute-start | bytes 49160 | tf_op jit(solution)/shard_map/ppermute | solution.py:492
  63.1 4.1 %student.1 = (bf16[512,768]{1,0:T(8,128)(2,1)S(1)}, bf16[512,768]{1,0:T(8,128)(2,1)S(1)}, bf16[768,512]{1,0:T(8,128)(2,1)S(1)}, f32[8,128]{1,0:T(8,128)S(1)}) custom-call(bf16[512,2048]{1,0:T(8,128)(2,1)S(1)} %get-tuple-element.110.se_ref, bf16[512,2048]{1,0:T(8,128)(2,1)S(1)} %get-tuple-element.111.sig_ref, ...), custom_call_target="tpu_custom_call" | custom-call | flops 1 | bytes 1 | tf_op jit(solution)/shard_map/student/pallas_call | solution.py:471
  68.0 4.1 %collective-permute-start.21 = (f32[8,512]{1,0:T(8,128)S(1)}, f32[8,512]{1,0:T(8,128)S(1)}, u32[]{:S(2)}, u32[]{:S(2)}) collective-permute-start(f32[8,512]{1,0:T(8,128)S(1)} %get-tuple-element.117.window_ref), channel_id=1, source_target_pairs={{0,160},{32,192},{64,224},{96,0},{128,32},{160,64},{192,96},{224,1... | collective-permute-start | bytes 49160 | tf_op jit(solution)/shard_map/ppermute | solution.py:501
  72.6 2.4 %teacher.1.b_ref = bf16[512,768]{1,0:T(8,128)(2,1)S(1)} custom-call(bf16[512,2048]{1,0:T(8,128)(2,1)S(1)} %get-tuple-element.120.te_ref, bf16[2048,768]{1,0:T(8,128)(2,1)S(1)} %get-tuple-element.112.stu_ref, f32[512,768]{1,0:T(8,128)S(1)} %get-tuple-element.113.simg_ref, f32[512,128]{1,0:T(8,128)S(1)} %get-tuple-element.114.inv_ref, ...), custom_call_target="tpu_custom_call" | custom-call | flops 1 | bytes 1 | tf_op jit(solution)/shard_map/teacher/pallas_call | solution.py:480
  75.0 3.9 %collective-permute-done.22.behind_ref = f32[8,512]{1,0:T(8,128)S(1)} collective-permute-done((f32[8,512]{1,0:T(8,128)S(1)}, f32[8,512]{1,0:T(8,128)S(1)}, u32[]{:S(2)}, u32[]{:S(2)}) %collective-permute-start.22) | collective-permute-done | bytes 16416 | tf_op jit(solution)/shard_map/ppermute | solution.py:502
  78.9 2.4 %away.1 = (f32[392,768]{1,0:T(8,128)S(1)}, bf16[512,768]{1,0:T(8,128)(2,1)S(1)}, bf16[512,768]{1,0:T(8,128)(2,1)S(1)}, f32[8,512]{1,0:T(8,128)S(1)}) custom-call(s32[4]{0:T(128)S(1)} %pad_add_fusion.place_ref, f32[8,512]{1,0:T(8,128)S(1)} %get-tuple-element.117.window_ref, f32[8,512]{1,0:T(8,128)S(1)} %collective-permute-done.21.ahead_ref, ...), custom_call_target="tpu_custom_call" | custom-call | flops 1 | bytes 1 | tf_op jit(solution)/shard_map/away/pallas_call | solution.py:504
  89.8 3.1 %collective-permute-done.24.p_ref = bf16[112,768]{1,0:T(8,128)(2,1)S(1)} collective-permute-done((bf16[112,768]{1,0:T(8,128)(2,1)S(1)}, bf16[112,768]{1,0:T(8,128)(2,1)S(1)}, u32[]{:S(2)}, u32[]{:S(2)}) %collective-permute-start.24) | collective-permute-done | bytes 172064 | tf_op jit(solution)/shard_map/ppermute | solution.py:535
  92.9 5.0 %collective-permute-done.26.r_ref = bf16[112,768]{1,0:T(8,128)(2,1)S(1)} collective-permute-done((bf16[112,768]{1,0:T(8,128)(2,1)S(1)}, bf16[112,768]{1,0:T(8,128)(2,1)S(1)}, u32[]{:S(2)}, u32[]{:S(2)}) %collective-permute-start.26) | collective-permute-done | bytes 172064 | tf_op jit(solution)/shard_map/ppermute | solution.py:535
  102.2 5.8 %collective-permute-done.29.r_ref = bf16[64,768]{1,0:T(8,128)(2,1)S(1)} collective-permute-done((bf16[64,768]{1,0:T(8,128)(2,1)S(1)}, bf16[64,768]{1,0:T(8,128)(2,1)S(1)}, u32[]{:S(2)}, u32[]{:S(2)}) %collective-permute-start.29) | collective-permute-done | bytes 98336 | tf_op jit(solution)/shard_map/ppermute | solution.py:553
  110.2 3.1 %collective-permute-done.30 = f32[48,768]{1,0:T(8,128)S(1)} collective-permute-done((f32[48,768]{1,0:T(8,128)S(1)}, f32[48,768]{1,0:T(8,128)S(1)}, u32[]{:S(2)}, u32[]{:S(2)}) %collective-permute-start.30) | collective-permute-done | bytes 147488 | tf_op jit(solution)/shard_map/ppermute | solution.py:556
  113.3 2.0 %collective-permute-done.31 = f32[48,768]{1,0:T(8,128)S(1)} collective-permute-done((f32[48,768]{1,0:T(8,128)S(1)}, f32[48,768]{1,0:T(8,128)S(1)}, u32[]{:S(2)}, u32[]{:S(2)}) %collective-permute-start.31) | collective-permute-done | bytes 147488 | tf_op jit(solution)/shard_map/ppermute | solution.py:555
  115.7 3.5 %collective-permute-start.33 = (bf16[48,768]{1,0:T(8,128)(2,1)S(1)}, bf16[48,768]{1,0:T(8,128)(2,1)S(1)}, u32[]{:S(2)}, u32[]{:S(2)}) collective-permute-start(bf16[48,768]{1,0:T(8,128)(2,1)S(1)} %get-tuple-element.142), channel_id=1, source_target_pairs={{0,96},{32,128},{64,160},{96,192},{128,224},{160,0},{192,32},{224,... | collective-permute-start | bytes 221192 | tf_op jit(solution)/shard_map/ppermute | solution.py:560
  (71 shorter events, 37.5 us)
Async XLA Ops:
  3.6 12.9 %collective-permute-start.7 = (bf16[128,1792]{1,0:T(8,128)(2,1)S(1)}, bf16[128,1792]{1,0:T(8,128)(2,1)S(1)}, u32[]{:S(2)}, u32[]{:S(2)}) collective-permute-start(bf16[128,1792]{1,0:T(8,128)(2,1)S(1)} %get-tuple-element.73.img_ref), channel_id=1, source_target_pairs={{0,32},{1,225},{32,64},{33,1},{64,96},{65,33},{96,128},{97,65},{12... | collective-permute-start | bytes 1376264 | tf_op jit(solution)/shard_map/ppermute | solution.py:392
  5.6 8.5 %collective-permute-start.4 = (bf16[64,1792]{1,0:T(8,128)(2,1)S(1)}, bf16[64,1792]{1,0:T(8,128)(2,1)S(1)}, u32[]{:S(2)}, u32[]{:S(2)}) collective-permute-start(bf16[64,1792]{1,0:T(8,128)(2,1)S(1)} %get-tuple-element.72.a_ref), channel_id=1, source_target_pairs={{0,2},{1,5},{2,16},{3,7},{4,6},{5,9},{6,20},{7,11},{8,10},{9,13},{... | collective-permute-start | bytes 688136 | tf_op jit(solution)/shard_map/ppermute | solution.py:388
  7.2 6.9 %collective-permute-start.5 = (bf16[64,1792]{1,0:T(8,128)(2,1)S(1)}, bf16[64,1792]{1,0:T(8,128)(2,1)S(1)}, u32[]{:S(2)}, u32[]{:S(2)}) collective-permute-start(bf16[64,1792]{1,0:T(8,128)(2,1)S(1)} %get-tuple-element.72.a_ref), channel_id=1, source_target_pairs={{0,18},{1,13},{2,0},{3,15},{4,22},{5,1},{6,4},{7,3},{8,26},{9,5},{... | collective-permute-start | bytes 688136 | tf_op jit(solution)/shard_map/ppermute | solution.py:388
  8.9 7.7 %collective-permute-start.6 = (bf16[64,1792]{1,0:T(8,128)(2,1)S(1)}, bf16[64,1792]{1,0:T(8,128)(2,1)S(1)}, u32[]{:S(2)}, u32[]{:S(2)}) collective-permute-start(bf16[64,1792]{1,0:T(8,128)(2,1)S(1)} %get-tuple-element.72.a_ref), channel_id=1, source_target_pairs={{0,16},{1,9},{2,18},{3,11},{4,20},{5,13},{6,22},{7,15},{8,24},{9,1... | collective-permute-start | bytes 688136 | tf_op jit(solution)/shard_map/ppermute | solution.py:388
  10.8 15.4 %collective-permute-start.8 = (bf16[128,1792]{1,0:T(8,128)(2,1)S(1)}, bf16[128,1792]{1,0:T(8,128)(2,1)S(1)}, u32[]{:S(2)}, u32[]{:S(2)}) collective-permute-start(bf16[128,1792]{1,0:T(8,128)(2,1)S(1)} %get-tuple-element.73.img_ref), channel_id=1, source_target_pairs={{0,64},{1,193},{32,96},{33,225},{64,128},{65,1},{96,160},{97,33},{... | collective-permute-start | bytes 1376264 | tf_op jit(solution)/shard_map/ppermute | solution.py:392
  16.6 15.3 %collective-permute-start.12 = (bf16[256,1792]{1,0:T(8,128)(2,1)S(1)}, bf16[256,1792]{1,0:T(8,128)(2,1)S(1)}, u32[]{:S(2)}, u32[]{:S(2)}) collective-permute-start(bf16[256,1792]{1,0:T(8,128)(2,1)S(1)} %column.1.refs_0_), channel_id=1, source_target_pairs={{0,4},{1,3},{2,6},{3,17},{4,8},{5,7},{6,10},{7,21},{8,12},{9,11},{... | collective-permute-start | bytes 2752520 | tf_op jit(solution)/shard_map/ppermute | solution.py:388
  26.5 20.5 %collective-permute-start.16 = (bf16[256,1792]{1,0:T(8,128)(2,1)S(1)}, bf16[256,1792]{1,0:T(8,128)(2,1)S(1)}, u32[]{:S(2)}, u32[]{:S(2)}) collective-permute-start(bf16[256,1792]{1,0:T(8,128)(2,1)S(1)} %column.1.refs_0_), channel_id=1, source_target_pairs={{0,12},{1,19},{2,14},{3,1},{4,0},{5,23},{6,2},{7,5},{8,4},{9,27},{... | collective-permute-start | bytes 2752520 | tf_op jit(solution)/shard_map/ppermute | solution.py:388
  27.1 15.8 %collective-permute-start.9 = (bf16[192,1792]{1,0:T(8,128)(2,1)S(1)}, bf16[192,1792]{1,0:T(8,128)(2,1)S(1)}, u32[]{:S(2)}, u32[]{:S(2)}) collective-permute-start(bf16[192,1792]{1,0:T(8,128)(2,1)S(1)} %get-tuple-element.75), channel_id=1, source_target_pairs={{0,64},{1,193},{32,96},{33,225},{64,128},{65,1},{96,160},{97,33},{... | collective-permute-start | bytes 2064392 | tf_op jit(solution)/shard_map/ppermute | solution.py:392
  29.5 19.7 %collective-permute-start.14 = (bf16[256,1792]{1,0:T(8,128)(2,1)S(1)}, bf16[256,1792]{1,0:T(8,128)(2,1)S(1)}, u32[]{:S(2)}, u32[]{:S(2)}) collective-permute-start(bf16[256,1792]{1,0:T(8,128)(2,1)S(1)} %column.1.refs_0_), channel_id=1, source_target_pairs={{0,1},{1,0},{2,3},{3,2},{4,5},{5,4},{6,7},{7,6},{8,9},{9,8},{10,11... | collective-permute-start | bytes 2752520 | tf_op jit(solution)/shard_map/ppermute | solution.py:362
  31.9 19.4 %collective-permute-start.15 = (bf16[256,1792]{1,0:T(8,128)(2,1)S(1)}, bf16[256,1792]{1,0:T(8,128)(2,1)S(1)}, u32[]{:S(2)}, u32[]{:S(2)}) collective-permute-start(bf16[256,1792]{1,0:T(8,128)(2,1)S(1)} %collective-permute-done.12.refs_0_), channel_id=1, source_target_pairs={{0,1},{1,0},{2,3},{3,2},{4,5},{5,4},{6,7},{7,6},{8,9},{9,8},{10,11... | collective-permute-start | bytes 2752520 | tf_op jit(solution)/shard_map/ppermute | solution.py:362
  33.0 20.9 %collective-permute-start.13 = (bf16[256,1792]{1,0:T(8,128)(2,1)S(1)}, bf16[256,1792]{1,0:T(8,128)(2,1)S(1)}, u32[]{:S(2)}, u32[]{:S(2)}) collective-permute-start(bf16[256,1792]{1,0:T(8,128)(2,1)S(1)} %collective-permute-done.12.refs_0_), channel_id=1, source_target_pairs={{0,4},{1,3},{2,6},{3,17},{4,8},{5,7},{6,10},{7,21},{8,12},{9,11},{... | collective-permute-start | bytes 2752520 | tf_op jit(solution)/shard_map/ppermute | solution.py:388
  46.9 7.4 %collective-permute-start.17 = (bf16[256,1792]{1,0:T(8,128)(2,1)S(1)}, bf16[256,1792]{1,0:T(8,128)(2,1)S(1)}, u32[]{:S(2)}, u32[]{:S(2)}) collective-permute-start(bf16[256,1792]{1,0:T(8,128)(2,1)S(1)} %collective-permute-done.16.refs_0_), channel_id=1, source_target_pairs={{0,1},{1,0},{2,3},{3,2},{4,5},{5,4},{6,7},{7,6},{8,9},{9,8},{10,11... | collective-permute-start | bytes 2752520 | tf_op jit(solution)/shard_map/ppermute | solution.py:362
  60.0 7.1 %collective-permute-start.19 = (f32[8,512]{1,0:T(8,128)S(1)}, f32[8,512]{1,0:T(8,128)S(1)}, u32[]{:S(2)}, u32[]{:S(2)}) collective-permute-start(f32[8,512]{1,0:T(8,128)S(1)} %get-tuple-element.109.own_ref.flat_ref), channel_id=1, source_target_pairs={{0,224},{32,0},{64,32},{96,64},{128,96},{160,128},{192,160},{224,1... | collective-permute-start | bytes 49160 | tf_op jit(solution)/shard_map/ppermute | solution.py:492
  68.0 7.0 %collective-permute-start.21 = (f32[8,512]{1,0:T(8,128)S(1)}, f32[8,512]{1,0:T(8,128)S(1)}, u32[]{:S(2)}, u32[]{:S(2)}) collective-permute-start(f32[8,512]{1,0:T(8,128)S(1)} %get-tuple-element.117.window_ref), channel_id=1, source_target_pairs={{0,160},{32,192},{64,224},{96,0},{128,32},{160,64},{192,96},{224,1... | collective-permute-start | bytes 49160 | tf_op jit(solution)/shard_map/ppermute | solution.py:501
  72.2 6.7 %collective-permute-start.22 = (f32[8,512]{1,0:T(8,128)S(1)}, f32[8,512]{1,0:T(8,128)S(1)}, u32[]{:S(2)}, u32[]{:S(2)}) collective-permute-start(f32[8,512]{1,0:T(8,128)S(1)} %get-tuple-element.118), channel_id=1, source_target_pairs={{0,96},{32,128},{64,160},{96,192},{128,224},{160,0},{192,32},{224,... | collective-permute-start | bytes 49160 | tf_op jit(solution)/shard_map/ppermute | solution.py:502
  84.9 8.0 %collective-permute-start.24 = (bf16[112,768]{1,0:T(8,128)(2,1)S(1)}, bf16[112,768]{1,0:T(8,128)(2,1)S(1)}, u32[]{:S(2)}, u32[]{:S(2)}) collective-permute-start(bf16[112,768]{1,0:T(8,128)(2,1)S(1)} %get-tuple-element.133), channel_id=1, source_target_pairs={{0,4},{4,8},{8,12},{12,0},{1,5},{5,9},{9,13},{13,1},{2,6},{6,10},{... | collective-permute-start | bytes 516104 | tf_op jit(solution)/shard_map/ppermute | solution.py:535
  86.5 6.4 %collective-permute-start.25 = (bf16[112,768]{1,0:T(8,128)(2,1)S(1)}, bf16[112,768]{1,0:T(8,128)(2,1)S(1)}, u32[]{:S(2)}, u32[]{:S(2)}) collective-permute-start(bf16[112,768]{1,0:T(8,128)(2,1)S(1)} %get-tuple-element.134), channel_id=1, source_target_pairs={{0,12},{4,0},{8,4},{12,8},{1,13},{5,1},{9,5},{13,9},{2,14},{6,2},{... | collective-permute-start | bytes 516104 | tf_op jit(solution)/shard_map/ppermute | solution.py:535
  87.8 10.1 %collective-permute-start.26 = (bf16[112,768]{1,0:T(8,128)(2,1)S(1)}, bf16[112,768]{1,0:T(8,128)(2,1)S(1)}, u32[]{:S(2)}, u32[]{:S(2)}) collective-permute-start(bf16[112,768]{1,0:T(8,128)(2,1)S(1)} %get-tuple-element.135), channel_id=1, source_target_pairs={{0,8},{4,12},{8,0},{12,4},{1,9},{5,13},{9,1},{13,5},{2,10},{6,14},... | collective-permute-start | bytes 516104 | tf_op jit(solution)/shard_map/ppermute | solution.py:535
  98.6 9.4 %collective-permute-start.27 = (f32[56,768]{1,0:T(8,128)S(1)}, f32[56,768]{1,0:T(8,128)S(1)}, u32[]{:S(2)}, u32[]{:S(2)}) collective-permute-start(f32[56,768]{1,0:T(8,128)S(1)} %get-tuple-element.137), channel_id=1, source_target_pairs={{0,2},{2,16},{16,18},{18,0},{1,3},{3,17},{17,19},{19,1},{4,6},{6,2... | collective-permute-start | bytes 516104 | tf_op jit(solution)/shard_map/ppermute | solution.py:553
  100.1 7.9 %collective-permute-start.28 = (f32[56,768]{1,0:T(8,128)S(1)}, f32[56,768]{1,0:T(8,128)S(1)}, u32[]{:S(2)}, u32[]{:S(2)}) collective-permute-start(f32[56,768]{1,0:T(8,128)S(1)} %get-tuple-element.137), channel_id=1, source_target_pairs={{0,18},{2,0},{16,2},{18,16},{1,19},{3,1},{17,3},{19,17},{4,22},{6,... | collective-permute-start | bytes 516104 | tf_op jit(solution)/shard_map/ppermute | solution.py:553
  101.9 6.1 %collective-permute-start.29 = (bf16[64,768]{1,0:T(8,128)(2,1)S(1)}, bf16[64,768]{1,0:T(8,128)(2,1)S(1)}, u32[]{:S(2)}, u32[]{:S(2)}) collective-permute-start(bf16[64,768]{1,0:T(8,128)(2,1)S(1)} %get-tuple-element.138), channel_id=1, source_target_pairs={{0,16},{2,18},{16,0},{18,2},{1,17},{3,19},{17,1},{19,3},{4,20},{6,... | collective-permute-start | bytes 294920 | tf_op jit(solution)/shard_map/ppermute | solution.py:553
  108.9 6.4 %collective-permute-start.31 = (f32[48,768]{1,0:T(8,128)S(1)}, f32[48,768]{1,0:T(8,128)S(1)}, u32[]{:S(2)}, u32[]{:S(2)}) collective-permute-start(f32[48,768]{1,0:T(8,128)S(1)} %get-tuple-element.140), channel_id=1, source_target_pairs={{0,32},{32,64},{64,96},{96,128},{128,160},{160,192},{192,224},{224... | collective-permute-start | bytes 442376 | tf_op jit(solution)/shard_map/ppermute | solution.py:555
  115.3 7.1 %collective-permute-start.32 = (bf16[48,768]{1,0:T(8,128)(2,1)S(1)}, bf16[48,768]{1,0:T(8,128)(2,1)S(1)}, u32[]{:S(2)}, u32[]{:S(2)}) collective-permute-start(bf16[48,768]{1,0:T(8,128)(2,1)S(1)} %get-tuple-element.141), channel_id=1, source_target_pairs={{0,160},{32,192},{64,224},{96,0},{128,32},{160,64},{192,96},{224,1... | collective-permute-start | bytes 221192 | tf_op jit(solution)/shard_map/ppermute | solution.py:559
  115.7 7.4 %collective-permute-start.33 = (bf16[48,768]{1,0:T(8,128)(2,1)S(1)}, bf16[48,768]{1,0:T(8,128)(2,1)S(1)}, u32[]{:S(2)}, u32[]{:S(2)}) collective-permute-start(bf16[48,768]{1,0:T(8,128)(2,1)S(1)} %get-tuple-element.142), channel_id=1, source_target_pairs={{0,96},{32,128},{64,160},{96,192},{128,224},{160,0},{192,32},{224,... | collective-permute-start | bytes 221192 | tf_op jit(solution)/shard_map/ppermute | solution.py:560
  (11 other events, 62.9 us)
